TPU v7x, 32 devices: a whole 2x2x4 slice. The times are simulated.
32 devices in a mesh: row: 4 (over z), col: 8 (over y, x, core).
Axes of the slice: x: 2, y: 2, z: 4, core: 2. Of those that a mesh axis runs over, the one named last changes fastest.
Arguments:
- amplitudes: float32 [1024, 20480], P('col', 'row'), may hold values from -6 to 6
- integrals: float32 [20480, 20480], P('row', 'col'), may hold values from -0.0390625 to 0.0390625
- occ_energy: float32 [64], replicated, may hold values from -1.5 to -0.25
- vir_energy: float32 [256], replicated, may hold values from 0.25 to 1.5
- occ_first: int32 [1024], P('row'), may hold values from 0 to 63
- occ_second: int32 [1024], P('row'), may hold values from 0 to 63
- vir_first: int32 [20480], P('col'), may hold values from 0 to 255
- vir_second: int32 [20480], P('col'), may hold values from 0 to 255
Outputs:
- update: float32 [1024, 20480], P('row', 'col')
All inputs are finite; a program needn't handle non-finite values.
Results may differ from a plain program's by a relative error of at most 0.00007.
Values sent between devices are 32-bit elements; how exact they have to be, the bound alone decides.
No kernel may reach another device: no remote copies, remote signals or barrier semaphores. Data moves between devices by JAX's collectives and lax.ppermute only.
A program may use at most 128 MiB of HBM per device.

v0:
```python
import jax
import jax.numpy as jnp
from jax import lax
from jax.sharding import PartitionSpec as P


def lookup(table, index):
    positions = jnp.arange(table.shape[0], dtype=jnp.int32)
    picked = jnp.where(index[:, None] == positions[None, :], table[None, :], jnp.float32(0.0))
    return jnp.sum(picked, axis=1)


def per_device(
    amplitudes, integrals, occ_energy, vir_energy, occ_first, occ_second, vir_first, vir_second
):
    partial_rows = jnp.dot(
        lax.all_gather(amplitudes, "col", axis=0, tiled=True),
        integrals,
        preferred_element_type=jnp.float32,
        precision=lax.Precision.HIGHEST,
    )
    ladder = lax.psum_scatter(partial_rows, "row", scatter_dimension=0, tiled=True)
    occ_sum = lookup(occ_energy, occ_first) + lookup(occ_energy, occ_second)
    vir_sum = lookup(vir_energy, vir_first) + lookup(vir_energy, vir_second)
    denom = vir_sum[None, :] - occ_sum[:, None]
    return ladder / denom


def solution(mesh):
    placed = (P("col", "row"), P("row", "col"), P(), P(), P("row"), P("row"), P("col"), P("col"))
    return jax.shard_map(
        per_device, mesh=mesh, in_specs=placed, out_specs=P("row", "col"), check_vma=False
    )
```

profile of v0, /device:TPU:0, one launch (start us, length us, event | category | flops | bytes accessed | tf_op | source)
XLA Modules:
  0.0 483.8 jit_solution(17952323415417162627)
XLA Ops:
  6.5 0.0 all-gather.2.cloned.1.call-start
  6.5 0.7 all-gather.2.cloned.1.call-update
  7.3 0.0 reduce-scatter.2.cloned.1.call-start
  7.3 112.3 %all-gather.2.cloned.1.call-done = f32[1024,5120]{1,0:T(8,128)} async-done(((f32[128,5120]{1,0:T(8,128)}), f32[1024,5120]{1,0:T(8,128)}) %all-gather.2.cloned.1.call-update) | async-done | bytes 20971536 | tf_op jit(solution)/shard_map/all_gather | solution.py:17
  119.6 175.5 %fusion = f32[1024,2560]{1,0:T(8,128)} fusion(f32[1024,5120]{1,0:T(8,128)} %all-gather.2.cloned.1.call-done, f32[5120,2560]{1,0:T(8,128)} %param.9), kind=kOutput, calls=%fused_computation.9 | convolution fusion | flops 161061273600 | bytes 83886080 | tf_op jit(solution)/shard_map/dot_general | solution.py:16
  295.1 0.0 copy-start.3
  295.1 0.0 copy-start.4
  295.1 0.0 copy-start.5
  295.1 0.0 copy-start
  295.1 0.0 copy-start.1
  295.1 0.0 copy-start.2
  295.1 0.0 reduce-scatter.2.cloned.1.call-update
  295.1 0.6 copy-done.3
  295.8 0.0 copy-done.4
  295.8 0.0 copy-done.5
  295.8 0.1 select_reduce_fusion.2
  295.9 0.0 copy-done
  295.9 0.0 copy-done.1
  295.9 0.0 copy-done.2
  295.9 2.3 select_reduce_fusion
  298.2 175.1 %reduce-scatter.2.cloned.1.call-done = f32[256,2560]{1,0:T(8,128)} async-done(((f32[1024,2560]{1,0:T(8,128)}), f32[256,2560]{1,0:T(8,128)}) %reduce-scatter.2.cloned.1.call-update) | async-done | bytes 2621456 | tf_op jit(solution)/shard_map/reduce_scatter | solution.py:22
  473.3 3.6 subtract_divide_fusion
  (2 shorter events, 0.0 us)
Async XLA Ops:
  6.5 113.0 %all-gather.2.cloned.1.call-start = ((), (), s32[]{:S(2)}) async-start(), calls=%async_computation.1 | async-start | bytes 23592960 | tf_op jit(solution)/shard_map/all_gather | solution.py:17
  7.3 466.1 %reduce-scatter.2.cloned.1.call-start = ((), (), s32[]{:S(2)}) async-start(), calls=%async_computation.2 | async-start | bytes 13107200 | tf_op jit(solution)/shard_map/reduce_scatter | solution.py:22
  295.1 0.7 copy-start.3
  295.1 0.7 copy-start.4
  295.1 0.7 copy-start.5
  295.1 0.8 copy-start
  295.1 0.8 copy-start.1
  295.1 0.8 copy-start.2
Sparse Core Ops, SparseCore 0:
  9.2 110.2 all-gather.1
  295.3 178.0 reduce-scatter.1
where the time goes:
time: 484 us
  waiting for transfers between devices  288 us (60%)
  matrix products  176 us (36%)
  between operations  13.5 us (3%)
  other arithmetic  6.06 us (1%)
    dot_general x1, matrix products, per_device(): jnp.dot(lax.all_gather(amplitudes, 'col', axis=0, tiled=True), integrals,...  176 us
    reduce_scatter x1, waiting for transfers between devices, per_device(): lax.psum_scatter(partial_rows, 'row', scatter_dimension=0, tiled=True)  175 us
    all_gather x1, waiting for transfers between devices, per_device(): lax.all_gather(amplitudes, 'col', axis=0, tiled=True)  112 us
  transfers between devices with their start and end apart: 2, of which 2 were waited for; matrix products, arithmetic and copies ran while one was open for 0% of the time, Pallas kernels for 0%

commit v1 on v0

v1 whole, which is shorter than its diff:
```python
import functools

import jax
import jax.numpy as jnp
from jax import lax
from jax.experimental import pallas as pl
from jax.experimental.pallas import tpu as pltpu
from jax.sharding import PartitionSpec as P

PLAN = ((1, (1, 1)), (1, (1,)), (1, (1,)), (1, (1, 1)))
TILE_BYTES = 5500000


def lookup(table, index):
    positions = jnp.arange(table.shape[0], dtype=jnp.int32)
    picked = jnp.where(index[:, None] == positions[None, :], table[None, :], jnp.float32(0.0))
    return jnp.sum(picked, axis=1)


def halves(values):
    high = values.astype(jnp.bfloat16)
    return high, (values - high.astype(jnp.float32)).astype(jnp.bfloat16)


def product_kernel(m, sources, cuts, place_ref, *refs):
    a_refs, b_ref = refs[:sources], refs[sources]
    out_refs, stacked = refs[sources + 1 : -1], refs[-1]
    rows = stacked.shape[0] // 2

    @pl.when(pl.program_id(0) == 0)
    def _():
        q = 0
        for a_ref in a_refs:
            for at in range(0, a_ref.shape[0], m):
                high, low = halves(a_ref[at : at + m, :])
                start = pl.multiple_of(place_ref[q] * m, m)
                stacked[pl.ds(start, m), :] = high
                stacked[pl.ds(rows + start, m), :] = low
                q += 1

    b_high, b_low = halves(b_ref[...])
    both = jnp.dot(stacked[...], b_high, preferred_element_type=jnp.float32)
    total = both[:rows] + (both[rows:] + jnp.dot(stacked[:rows, :], b_low, preferred_element_type=jnp.float32))
    for out_ref, (first, last) in zip(out_refs, cuts):
        out_ref[...] = total[first:last]


def column_tile(depth, columns, offset):
    best = 128
    for tile in range(128, columns + 1, 128):
        if columns % tile == 0 and offset % tile == 0 and depth * tile * 4 <= TILE_BYTES:
            best = tile
    return best


def product(place, sources, m, integrals, offset, columns, cuts):
    depth = integrals.shape[0]
    rows = m * place.shape[0]
    tile = column_tile(depth, columns, offset)
    return pl.pallas_call(
        functools.partial(product_kernel, m, len(sources), cuts),
        grid=(columns // tile,),
        in_specs=[pl.BlockSpec(memory_space=pltpu.SMEM)]
        + [pl.BlockSpec(source.shape, lambda j: (0, 0), pipeline_mode=pl.Buffered(1)) for source in sources]
        + [pl.BlockSpec((depth, tile), lambda j: (0, j + offset // tile))],
        out_specs=[pl.BlockSpec((last - first, tile), lambda j: (0, j)) for first, last in cuts],
        out_shape=[jax.ShapeDtypeStruct((last - first, columns), jnp.float32) for first, last in cuts],
        scratch_shapes=[pltpu.VMEM((2 * rows, depth), jnp.bfloat16)],
        compiler_params=pltpu.CompilerParams(vmem_limit_bytes=58 * 2**20),
        cost_estimate=pl.CostEstimate(
            flops=6 * rows * depth * columns, bytes_accessed=4 * (depth * columns + rows * (depth + columns)), transcendentals=0
        ),
        name="ladder_product",
    )(place, *sources, integrals)


def across(block, axis, bits, size):
    return lax.ppermute(block, axis, [(i, i ^ bits) for i in range(size)])


def row_parts(own):
    if own % 16:
        return [(0, own, (1,))]
    total = sum(share for share, _ in PLAN)
    out, at, so_far = [], 0, 0
    for share, pieces in PLAN:
        so_far += share
        end = own * so_far // total // 16 * 16
        if end > at:
            out.append((at, end, pieces))
            at = end
    return out


def column_pieces(columns, pieces):
    out, at, so_far = [], 0, 0
    for share in pieces:
        so_far += share
        end = columns * so_far // sum(pieces) // 256 * 256 if so_far < sum(pieces) else columns
        if end > at:
            out.append((at, end - at))
            at = end
    return out


def plain(amplitudes, integrals):
    rows = jnp.dot(
        lax.all_gather(amplitudes, "col", axis=0, tiled=True),
        integrals,
        preferred_element_type=jnp.float32,
        precision=lax.Precision.HIGHEST,
    )
    return lax.psum_scatter(rows, "row", scatter_dimension=0, tiled=True)


class Steps:
    def __init__(self):
        self.held, self.due = {}, {}

    def post(self, key, value, step):
        self.held[key] = value
        self.due.setdefault(step, []).append(key)

    def settle(self, step, value):
        keys = self.due.pop(step, [])
        value, held = lax.optimization_barrier((value, [self.held[key] for key in keys]))
        self.held.update(zip(keys, held))
        return value


def per_device(
    size, col_size, amplitudes, integrals, occ_energy, vir_energy, occ_first, occ_second, vir_first, vir_second
):
    own, columns = amplitudes.shape[0], integrals.shape[1]
    if size & (size - 1) or col_size & (col_size - 1) or col_size % size or columns % 128 or own % 8:
        occ_sum = lookup(occ_energy, occ_first) + lookup(occ_energy, occ_second)
        vir_sum = lookup(vir_energy, vir_first) + lookup(vir_energy, vir_second)
        return plain(amplitudes, integrals) / (vir_sum[None, :] - occ_sum[:, None])
    group = col_size // size
    rounds = size.bit_length() - 1
    order = lax.axis_index("col") ^ jnp.arange(col_size, dtype=jnp.int32)
    differs, owner = lax.axis_index("row") ^ (order // group), 0
    for bit in range(rounds):
        owner = owner * 2 + (differs >> bit) % 2
    place = owner * group + order % group

    parts = row_parts(own)
    todo = []
    for number, (first, last, pieces) in enumerate(parts):
        pieces = column_pieces(columns, pieces)
        for piece, (offset, width) in enumerate(pieces):
            todo.append((number, piece, len(pieces), first, last, offset, width))
    count = len(todo)
    steps = Steps()
    held = steps.held
    evens = list(range(0, col_size, 2))

    def gather(number, wanted, due):
        for q in wanted:
            source, bits = (0, q) if q % 2 == 0 else (q - 1, 1)
            steps.post((number, q), across(held[number, source], "col", bits, col_size), due)

    def send(p, turn):
        _, _, _, first, last, _, _ = todo[p]
        block = group * (last - first)
        half = size // 2**turn // 2 * block
        if turn == 0:
            return across(made[p][1], "row", 1, size)
        values = held["sum", p, turn - 1][half:]
        kept = made[p][0][half : 2 * half]
        for earlier in range(turn - 1):
            kept = kept + held["sum", p, earlier][half : 2 * half]
        return across(values + kept, "row", 2**turn, size)

    def write(update, p):
        _, _, _, first, last, offset, width = todo[p]
        block = group * (last - first)
        ladder = made[p][0][:block]
        for turn in range(rounds):
            ladder = ladder + held["sum", p, turn][:block]
        denom = vir_sum[None, None, offset : offset + width] - occ_sum[:, first:last, None]
        written.add(p)
        return lax.dynamic_update_slice(update, ladder.reshape(group, last - first, width) / denom, (0, first, offset))

    made, written = {}, set()
    held[0, 0] = amplitudes[parts[0][0] : parts[0][1]]
    gather(0, evens[1:], 0)
    gather(0, [q + 1 for q in evens], 0)
    terms_at = min(1, count - 1)
    for step in range(count + 1):
        if step == terms_at:
            steps.post("terms", (vir_first, vir_second, occ_first, occ_second), step)
        place = steps.settle(step, place)
        if step == terms_at:
            vir_first, vir_second, occ_first, occ_second = held["terms"]
            occ_sum = (lookup(occ_energy, occ_first) + lookup(occ_energy, occ_second)).reshape(group, own)
            vir_sum = lookup(vir_energy, vir_first) + lookup(vir_energy, vir_second)
            steps.post("denominators", (occ_sum, vir_sum, jnp.zeros((group, own, columns), jnp.float32)), step + 1)
        if step > terms_at:
            occ_sum, vir_sum, update = held["denominators"]
        if step == count:
            break
        number, piece, pieces, first, last, offset, width = todo[step]
        m = last - first
        block = group * m
        if number + 1 < len(parts):
            if piece == 0:
                held[number + 1, 0] = amplitudes[parts[number + 1][0] : parts[number + 1][1]]
                gather(number + 1, [1], step + 1)
            cut = [evens[1:][(col_size // 2 - 1) * k // pieces : (col_size // 2 - 1) * (k + 1) // pieces] for k in range(pieces)][::-1]
            gather(number + 1, cut[piece], step + 1)
            if piece:
                gather(number + 1, [q + 1 for q in cut[piece - 1]], step + 1)
        if piece == 0 and number:
            gather(number, [q + 1 for q in evens if (number, q + 1) not in held], step)
        for p in range(step):
            turn = step - 1 - p
            if 0 < turn < rounds:
                steps.post(("sum", p, turn), send(p, turn), step + 1)
            if turn == rounds and step > terms_at:
                update = write(update, p)
                steps.post("denominators", (occ_sum, vir_sum, update), step + 1)
        sources = [held[number, q] for q in range(col_size)]
        cuts = [(0, size // 2 * block), (size // 2 * block, size * block)] if size > 1 else [(0, block)]
        made[step] = product(place, sources, m, integrals, offset, width, cuts)
        steps.post(("made", step), made[step], step + 1)
        if rounds:
            steps.post(("sum", step, 0), send(step, 0), step + 2)
    for turn in range(1, rounds):
        for p in range(count):
            if ("sum", p, turn) not in held:
                held["sum", p, turn] = send(p, turn)
    for p in range(count):
        if p not in written:
            update = write(update, p)
    return update.reshape(group * own, columns)


def solution(mesh):
    placed = (P("col", "row"), P("row", "col"), P(), P(), P("row"), P("row"), P("col"), P("col"))
    return jax.shard_map(
        functools.partial(per_device, mesh.shape["row"], mesh.shape["col"]),
        mesh=mesh,
        in_specs=placed,
        out_specs=P("row", "col"),
        check_vma=False,
    )
```

time: 484 us -> 279 us (0.58)
  waiting for transfers between devices: 288 us -> 96.7 us
  matrix products: 176 us -> 0 us
  Pallas kernels: 0 us -> 128 us
  starting transfers between devices: 0.04 us -> 29.5 us
  between operations: 13.5 us -> 0.58 us
  other arithmetic: 6.06 us -> 14.6 us
  local copies, waits for them, and re-layouts: 0.65 us -> 7.37 us
    dot_general x1 -> x0, matrix products: 176 us -> none  [per_device(): jnp.dot(lax.all_gather(amplitudes, 'col', axis=0, tiled=True), integrals,...]
    reduce_scatter x1 -> x0, waiting for transfers between devices: 175 us -> none  [per_device(): lax.psum_scatter(partial_rows, 'row', scatter_dimension=0, tiled=True)]
    pallas_call x0 -> x6, Pallas kernels: none -> 128 us  [product(): pl.pallas_call(functools.partial(product_kernel, m, len(sources), cuts),...]
    all_gather x1 -> x0, waiting for transfers between devices: 112 us -> none  [per_device(): lax.all_gather(amplitudes, 'col', axis=0, tiled=True)]
    ppermute x0 -> x40, waiting for transfers between devices: none -> 96.7 us  [across(): return lax.ppermute(block, axis, [(i, i ^ bits) for i in range(size)])]
    ppermute x0 -> x40, starting transfers between devices: none -> 29.5 us  [across(): return lax.ppermute(block, axis, [(i, i ^ bits) for i in range(size)])]
    add x1 -> x14, other arithmetic: 0.01 us -> 7.54 us  [the longest x6 3.63 us: write(): ladder = ladder + held['sum', p, turn][:block]]
  transfers between devices with their start and end apart: 2 -> 40, of which waited for: 2 -> 9; matrix products, arithmetic and copies ran while one was open for 0% -> 5% of each run, Pallas kernels for 0% -> 46%
where the time goes in v1:
time: 279 us; the launch traced here: 277 us
  Pallas kernels  128 us (46%)
  waiting for transfers between devices  96.7 us (35%)
  starting transfers between devices  29.5 us (11%)
  other arithmetic  14.6 us (5%)
  local copies, waits for them, and re-layouts  7.37 us (3%)
    pallas_call x6, Pallas kernels, product(): pl.pallas_call(functools.partial(product_kernel, m, len(sources), cuts),...  128 us
    ppermute x40, waiting for transfers between devices, across(): return lax.ppermute(block, axis, [(i, i ^ bits) for i in range(size)])  96.7 us
    ppermute x40, starting transfers between devices, across(): return lax.ppermute(block, axis, [(i, i ^ bits) for i in range(size)])  29.5 us
  transfers between devices with their start and end apart: 40, of which 9 were waited for; matrix products, arithmetic and copies ran while one was open for 5% of the time, Pallas kernels for 46%

profile of v1, /device:TPU:0, one launch (start us, length us, event | category | flops | bytes accessed | tf_op | source)
XLA Modules:
  0.0 277.2 jit_solution(12718514544888153102)
XLA Ops:
  0.0 3.0 %fusion.6 = (f32[32,5120]{1,0:T(8,128)S(1)}, f32[32,5120]{1,0:T(8,128)}, f32[32,5120]{1,0:T(8,128)S(1)}, f32[32,5120]{1,0:T(8,128)}) fusion(f32[128,5120]{1,0:T(8,128)} %param.8), kind=kLoop, calls=%fused_computation.44 | loop fusion | bytes 5242880 | tf_op jit(solution)/shard_map/slice | solution.py:208
  3.0 2.9 %collective-permute-start = (f32[32,5120]{1,0:T(8,128)S(1)}, f32[32,5120]{1,0:T(8,128)S(1)}, u32[]{:S(2)}, u32[]{:S(2)}) collective-permute-start(f32[32,5120]{1,0:T(8,128)S(1)} %get-tuple-element.139.refs_0_), channel_id=1, source_target_pairs={{0,2},{1,3},{2,0},{3,1},{4,6},{5,7},{6,4},{7,5},{8,10},{9,11},{10,... | collective-permute-start | bytes 1966088 | tf_op jit(solution)/shard_map/ppermute | solution.py:78
  5.9 1.5 collective-permute-start.1
  7.4 14.0 %collective-permute-done.refs_2_ = f32[32,5120]{1,0:T(8,128)S(1)} collective-permute-done((f32[32,5120]{1,0:T(8,128)S(1)}, f32[32,5120]{1,0:T(8,128)S(1)}, u32[]{:S(2)}, u32[]{:S(2)}) %collective-permute-start) | collective-permute-done | bytes 655392 | tf_op jit(solution)/shard_map/ppermute | solution.py:78
  21.5 14.7 %collective-permute-done.1.refs_4_ = f32[32,5120]{1,0:T(8,128)S(1)} collective-permute-done((f32[32,5120]{1,0:T(8,128)S(1)}, f32[32,5120]{1,0:T(8,128)S(1)}, u32[]{:S(2)}, u32[]{:S(2)}) %collective-permute-start.1) | collective-permute-done | bytes 655392 | tf_op jit(solution)/shard_map/ppermute | solution.py:78
  36.2 0.5 collective-permute-start.6
  36.7 0.1 collective-permute-start.7
  36.7 0.5 fusion.2.place_ref
  37.3 1.5 collective-permute-start.8
  38.8 1.1 collective-permute-start.9
  39.9 0.9 collective-permute-start.11
  40.8 0.1 collective-permute-start.15
  41.0 17.4 %ladder_product.6 = (f32[128,1280]{1,0:T(8,128)}, f32[128,1280]{1,0:T(8,128)}) custom-call(s32[8]{0:T(128)} %fusion.2.place_ref, f32[32,5120]{1,0:T(8,128)} %copy-done.1, f32[32,5120]{1,0:T(8,128)} %collective-permute-done.3.refs_1_, f32[32,5120]{1,0:T(8,128)} %copy-done.4, f32[32,5120]{1,0:T(8,128)} %collective-permute-done.4.refs_3_, ...), custom_call_target="tpu_custom_call" | custom-call | flops 10066329600 | bytes 32768000 | tf_op jit(solution)/shard_map/ladder_product/pallas_call | solution.py:60
  58.3 1.6 collective-permute-start.10
  60.0 8.7 %collective-permute-done.8.refs_4_ = f32[32,5120]{1,0:T(8,128)S(1)} collective-permute-done((f32[32,5120]{1,0:T(8,128)}, f32[32,5120]{1,0:T(8,128)S(1)}, u32[]{:S(2)}, u32[]{:S(2)}) %collective-permute-start.8) | collective-permute-done | bytes 655392 | tf_op jit(solution)/shard_map/ppermute | solution.py:78
  68.7 0.5 collective-permute-start.13
  69.2 0.1 select_reduce_fusion.2
  69.4 2.3 select_reduce_fusion
  71.7 17.5 %ladder_product.7 = (f32[128,1280]{1,0:T(8,128)}, f32[128,1280]{1,0:T(8,128)}) custom-call(s32[8]{0:T(128)} %fusion.2.place_ref, f32[32,5120]{1,0:T(8,128)} %copy-done.1, f32[32,5120]{1,0:T(8,128)} %collective-permute-done.3.refs_1_, f32[32,5120]{1,0:T(8,128)} %copy-done.4, f32[32,5120]{1,0:T(8,128)} %collective-permute-done.4.refs_3_, ...), custom_call_target="tpu_custom_call" | custom-call | flops 10066329600 | bytes 32768000 | tf_op jit(solution)/shard_map/ladder_product/pallas_call | solution.py:60
  89.3 0.1 collective-permute-start.20
  89.4 0.7 collective-permute-start.16
  90.1 1.3 collective-permute-start.17
  91.5 1.4 collective-permute-start.18
  93.0 1.6 collective-permute-start.14
  94.6 2.6 collective-permute-start.19
  97.2 29.5 %ladder_product.8 = (f32[128,2560]{1,0:T(8,128)}, f32[128,2560]{1,0:T(8,128)}) custom-call(s32[8]{0:T(128)} %fusion.2.place_ref, f32[32,5120]{1,0:T(8,128)} %get-tuple-element.138.refs_0_, f32[32,5120]{1,0:T(8,128)} %collective-permute-done.7.refs_1_, f32[32,5120]{1,0:T(8,128)} %collective-permute-done.11.refs_2_, ...), custom_call_target="tpu_custom_call" | custom-call | flops 20132659200 | bytes 60293120 | tf_op jit(solution)/shard_map/ladder_product/pallas_call | solution.py:60
  126.8 0.8 copy-done.31
  127.6 0.7 collective-permute-start.23
  128.4 0.5 collective-permute-start.28
  128.9 0.1 collective-permute-start.29
  129.0 0.3 broadcast_in_dim.38
  129.3 0.1 divide_dynamic-update-slice_fusion.5
  129.5 1.4 collective-permute-start.24
  131.0 2.3 collective-permute-start.25
  133.3 0.5 collective-permute-start.21
  133.8 0.3 copy-done.35
  134.1 0.8 copy-done.36
  135.0 0.3 collective-permute-start.26
  135.3 29.4 %ladder_product.9 = (f32[128,2560]{1,0:T(8,128)}, f32[128,2560]{1,0:T(8,128)}) custom-call(s32[8]{0:T(128)} %fusion.2.place_ref, f32[32,5120]{1,0:T(8,128)} %get-tuple-element.140.refs_0_, f32[32,5120]{1,0:T(8,128)} %collective-permute-done.15.refs_1_, f32[32,5120]{1,0:T(8,128)} %copy-done.31, f32[32,5120]{1,0:T(8,128)} %collective-permute-done.27.refs_3_, ...), custom_call_target="tpu_custom_call" | custom-call | flops 20132659200 | bytes 60293120 | tf_op jit(solution)/shard_map/ladder_product/pallas_call | solution.py:60
  164.7 1.3 collective-permute-start.30
  166.0 4.2 %collective-permute-done.26 = f32[64,1280]{1,0:T(8,128)S(1)} collective-permute-done((f32[64,1280]{1,0:T(8,128)S(1)}, f32[64,1280]{1,0:T(8,128)S(1)}, u32[]{:S(2)}, u32[]{:S(2)}) %collective-permute-start.26) | collective-permute-done | bytes 327712 | tf_op jit(solution)/shard_map/ppermute | solution.py:78
  170.2 2.1 collective-permute-done.21
  172.3 2.1 slice_add_fusion.1
  174.4 0.5 collective-permute-start.33
  174.9 1.1 add_add_fusion.3
  176.1 1.4 collective-permute-start.31
  177.5 0.8 divide_dynamic-update-slice_fusion.4
  178.4 0.8 copy-done.9
  179.2 0.2 copy-done.10
  179.4 0.8 copy-done.11
  180.3 17.4 %ladder_product.10 = (f32[128,1280]{1,0:T(8,128)}, f32[128,1280]{1,0:T(8,128)}) custom-call(s32[8]{0:T(128)} %fusion.2.place_ref, f32[32,5120]{1,0:T(8,128)} %copy-done, f32[32,5120]{1,0:T(8,128)} %copy-done.2, f32[32,5120]{1,0:T(8,128)} %copy-done.3, f32[32,5120]{1,0:T(8,128)} %copy-done.9, f32[32,5120]{1,0:T(8,128)} %copy-done.5, f32[32,5120]{1,0:T(8,128)} %copy-done.10, ...), custom_call_target="tpu_custom_call" | custom-call | flops 10066329600 | bytes 32768000 | tf_op jit(solution)/shard_map/ladder_product/pallas_call | solution.py:60
  197.7 16.8 %collective-permute-done.30 = f32[128,2560]{1,0:T(8,128)} collective-permute-done((f32[128,2560]{1,0:T(8,128)}, f32[128,2560]{1,0:T(8,128)}, u32[]{:S(2)}, u32[]{:S(2)}) %collective-permute-start.30) | collective-permute-done | bytes 1310752 | tf_op jit(solution)/shard_map/ppermute | solution.py:78
  214.5 1.2 add_add_fusion.1
  215.7 1.2 slice_add_fusion
  216.9 1.3 collective-permute-start.36
  218.2 17.4 %ladder_product.11 = (f32[128,1280]{1,0:T(8,128)}, f32[128,1280]{1,0:T(8,128)}) custom-call(s32[8]{0:T(128)} %fusion.2.place_ref, f32[32,5120]{1,0:T(8,128)} %copy-done, f32[32,5120]{1,0:T(8,128)} %copy-done.2, f32[32,5120]{1,0:T(8,128)} %copy-done.3, f32[32,5120]{1,0:T(8,128)} %copy-done.9, f32[32,5120]{1,0:T(8,128)} %copy-done.5, f32[32,5120]{1,0:T(8,128)} %copy-done.10, ...), custom_call_target="tpu_custom_call" | custom-call | flops 10066329600 | bytes 32768000 | tf_op jit(solution)/shard_map/ladder_product/pallas_call | solution.py:60
  235.6 1.0 divide_dynamic-update-slice_fusion.1
  236.6 9.9 %collective-permute-done.36 = f32[64,2560]{1,0:T(8,128)S(1)} collective-permute-done((f32[64,2560]{1,0:T(8,128)S(1)}, f32[64,2560]{1,0:T(8,128)S(1)}, u32[]{:S(2)}, u32[]{:S(2)}) %collective-permute-start.36) | collective-permute-done | bytes 655392 | tf_op jit(solution)/shard_map/ppermute | solution.py:78
  246.8 1.2 add_add_fusion
  247.9 14.5 %collective-permute-done.38 = f32[128,1280]{1,0:T(8,128)S(1)} collective-permute-done((f32[128,1280]{1,0:T(8,128)}, f32[128,1280]{1,0:T(8,128)S(1)}, u32[]{:S(2)}, u32[]{:S(2)}) %collective-permute-start.38) | collective-permute-done | bytes 655392 | tf_op jit(solution)/shard_map/ppermute | solution.py:78
  262.5 1.0 divide_dynamic-update-slice_fusion
  263.6 0.8 divide_dynamic-update-slice_fusion.3
  264.4 11.8 %collective-permute-done.39 = f32[64,1280]{1,0:T(8,128)S(1)} collective-permute-done((f32[64,1280]{1,0:T(8,128)S(1)}, f32[64,1280]{1,0:T(8,128)S(1)}, u32[]{:S(2)}, u32[]{:S(2)}) %collective-permute-start.39) | collective-permute-done | bytes 327712 | tf_op jit(solution)/shard_map/ppermute | solution.py:78
  276.3 0.8 divide_dynamic-update-slice_fusion.2
  (127 shorter events, 1.2 us)
Async XLA Ops:
  3.0 38.0 %copy-start.1 = (f32[32,5120]{1,0:T(8,128)}, f32[32,5120]{1,0:T(8,128)S(1)}, u32[]{:S(2)}) copy-start(f32[32,5120]{1,0:T(8,128)S(1)} %get-tuple-element.139.refs_0_) | copy-start | bytes 1966084
  3.0 128.0 %copy-start = (f32[32,5120]{1,0:T(8,128)}, f32[32,5120]{1,0:T(8,128)S(1)}, u32[]{:S(2)}) copy-start(f32[32,5120]{1,0:T(8,128)S(1)} %get-tuple-element.137.refs_0_) | copy-start | bytes 1966084
  3.0 18.5 %collective-permute-start = (f32[32,5120]{1,0:T(8,128)S(1)}, f32[32,5120]{1,0:T(8,128)S(1)}, u32[]{:S(2)}, u32[]{:S(2)}) collective-permute-start(f32[32,5120]{1,0:T(8,128)S(1)} %get-tuple-element.139.refs_0_), channel_id=1, source_target_pairs={{0,2},{1,3},{2,0},{3,1},{4,6},{5,7},{6,4},{7,5},{8,10},{9,11},{10,... | collective-permute-start | bytes 1966088 | tf_op jit(solution)/shard_map/ppermute | solution.py:78
  5.9 30.2 %collective-permute-start.1 = (f32[32,5120]{1,0:T(8,128)S(1)}, f32[32,5120]{1,0:T(8,128)S(1)}, u32[]{:S(2)}, u32[]{:S(2)}) collective-permute-start(f32[32,5120]{1,0:T(8,128)S(1)} %get-tuple-element.139.refs_0_), channel_id=1, source_target_pairs={{0,4},{1,5},{2,6},{3,7},{4,0},{5,1},{6,2},{7,3},{8,12},{9,13},{10,... | collective-permute-start | bytes 1966088 | tf_op jit(solution)/shard_map/ppermute | solution.py:78
  7.4 28.7 %collective-permute-start.2 = (f32[32,5120]{1,0:T(8,128)S(1)}, f32[32,5120]{1,0:T(8,128)S(1)}, u32[]{:S(2)}, u32[]{:S(2)}) collective-permute-start(f32[32,5120]{1,0:T(8,128)S(1)} %get-tuple-element.139.refs_0_), channel_id=1, source_target_pairs={{0,6},{1,7},{2,4},{3,5},{4,2},{5,3},{6,0},{7,1},{8,14},{9,15},{10,... | collective-permute-start | bytes 1966088 | tf_op jit(solution)/shard_map/ppermute | solution.py:78
  7.4 29.8 %collective-permute-start.3 = (f32[32,5120]{1,0:T(8,128)S(1)}, f32[32,5120]{1,0:T(8,128)}, u32[]{:S(2)}, u32[]{:S(2)}) collective-permute-start(f32[32,5120]{1,0:T(8,128)S(1)} %get-tuple-element.139.refs_0_), channel_id=1, source_target_pairs={{0,1},{1,0},{2,3},{3,2},{4,5},{5,4},{6,7},{7,6},{8,9},{9,8},{10,11... | collective-permute-start | bytes 1966088 | tf_op jit(solution)/shard_map/ppermute | solution.py:78
  21.5 19.5 %copy-start.4 = (f32[32,5120]{1,0:T(8,128)}, f32[32,5120]{1,0:T(8,128)S(1)}, u32[]{:S(2)}) copy-start(f32[32,5120]{1,0:T(8,128)S(1)} %collective-permute-done.refs_2_) | copy-start | bytes 1966084
  21.5 17.3 %collective-permute-start.4 = (f32[32,5120]{1,0:T(8,128)S(1)}, f32[32,5120]{1,0:T(8,128)}, u32[]{:S(2)}, u32[]{:S(2)}) collective-permute-start(f32[32,5120]{1,0:T(8,128)S(1)} %collective-permute-done.refs_2_), channel_id=1, source_target_pairs={{0,1},{1,0},{2,3},{3,2},{4,5},{5,4},{6,7},{7,6},{8,9},{9,8},{10,11... | collective-permute-start | bytes 1966088 | tf_op jit(solution)/shard_map/ppermute | solution.py:78
  36.1 3.8 %collective-permute-start.5 = (f32[32,5120]{1,0:T(8,128)S(1)}, f32[32,5120]{1,0:T(8,128)}, u32[]{:S(2)}, u32[]{:S(2)}) collective-permute-start(f32[32,5120]{1,0:T(8,128)S(1)} %collective-permute-done.1.refs_4_), channel_id=1, source_target_pairs={{0,1},{1,0},{2,3},{3,2},{4,5},{5,4},{6,7},{7,6},{8,9},{9,8},{10,11... | collective-permute-start | bytes 1966088 | tf_op jit(solution)/shard_map/ppermute | solution.py:78
  36.2 4.6 %collective-permute-start.6 = (f32[32,5120]{1,0:T(8,128)S(1)}, f32[32,5120]{1,0:T(8,128)}, u32[]{:S(2)}, u32[]{:S(2)}) collective-permute-start(f32[32,5120]{1,0:T(8,128)S(1)} %collective-permute-done.2.refs_6_), channel_id=1, source_target_pairs={{0,1},{1,0},{2,3},{3,2},{4,5},{5,4},{6,7},{7,6},{8,9},{9,8},{10,11... | collective-permute-start | bytes 1966088 | tf_op jit(solution)/shard_map/ppermute | solution.py:78
  36.7 21.7 %collective-permute-start.7 = (f32[32,5120]{1,0:T(8,128)}, f32[32,5120]{1,0:T(8,128)}, u32[]{:S(2)}, u32[]{:S(2)}) collective-permute-start(f32[32,5120]{1,0:T(8,128)} %get-tuple-element.138.refs_0_), channel_id=1, source_target_pairs={{0,1},{1,0},{2,3},{3,2},{4,5},{5,4},{6,7},{7,6},{8,9},{9,8},{10,11... | collective-permute-start | bytes 1966088 | tf_op jit(solution)/shard_map/ppermute | solution.py:78
  37.3 31.3 %collective-permute-start.8 = (f32[32,5120]{1,0:T(8,128)}, f32[32,5120]{1,0:T(8,128)S(1)}, u32[]{:S(2)}, u32[]{:S(2)}) collective-permute-start(f32[32,5120]{1,0:T(8,128)} %get-tuple-element.138.refs_0_), channel_id=1, source_target_pairs={{0,4},{1,5},{2,6},{3,7},{4,0},{5,1},{6,2},{7,3},{8,12},{9,13},{10,... | collective-permute-start | bytes 1966088 | tf_op jit(solution)/shard_map/ppermute | solution.py:78
  38.8 29.8 %collective-permute-start.9 = (f32[32,5120]{1,0:T(8,128)}, f32[32,5120]{1,0:T(8,128)S(1)}, u32[]{:S(2)}, u32[]{:S(2)}) collective-permute-start(f32[32,5120]{1,0:T(8,128)} %get-tuple-element.138.refs_0_), channel_id=1, source_target_pairs={{0,6},{1,7},{2,4},{3,5},{4,2},{5,3},{6,0},{7,1},{8,14},{9,15},{10,... | collective-permute-start | bytes 1966088 | tf_op jit(solution)/shard_map/ppermute | solution.py:78
  39.9 49.3 %collective-permute-start.11 = (f32[32,5120]{1,0:T(8,128)}, f32[32,5120]{1,0:T(8,128)}, u32[]{:S(2)}, u32[]{:S(2)}) collective-permute-start(f32[32,5120]{1,0:T(8,128)} %get-tuple-element.138.refs_0_), channel_id=1, source_target_pairs={{0,2},{1,3},{2,0},{3,1},{4,6},{5,7},{6,4},{7,5},{8,10},{9,11},{10,... | collective-permute-start | bytes 1966088 | tf_op jit(solution)/shard_map/ppermute | solution.py:78
  40.8 28.4 %copy-start.27 = (s32[256]{0:T(256)S(1)}, s32[256]{0:T(256)}, u32[]{:S(2)}) copy-start(s32[256]{0:T(256)} %param.13) | copy-start | bytes 3076
  40.8 28.4 %copy-start.28 = (s32[256]{0:T(256)S(1)}, s32[256]{0:T(256)}, u32[]{:S(2)}) copy-start(s32[256]{0:T(256)} %param.12) | copy-start | bytes 3076
  40.8 28.4 %copy-start.29 = (f32[64]{0:T(128)S(1)}, f32[64]{0:T(128)}, u32[]{:S(2)}) copy-start(f32[64]{0:T(128)} %param.10) | copy-start | bytes 772
  40.8 28.5 %copy-start.24 = (s32[2560]{0:T(1024)S(1)}, s32[2560]{0:T(1024)}, u32[]{:S(2)}) copy-start(s32[2560]{0:T(1024)} %param.15) | copy-start | bytes 30724
  40.8 28.5 %copy-start.25 = (s32[2560]{0:T(1024)S(1)}, s32[2560]{0:T(1024)}, u32[]{:S(2)}) copy-start(s32[2560]{0:T(1024)} %param.14) | copy-start | bytes 30724
  40.8 28.5 %copy-start.26 = (f32[256]{0:T(256)S(1)}, f32[256]{0:T(256)}, u32[]{:S(2)}) copy-start(f32[256]{0:T(256)} %param.11) | copy-start | bytes 3076
  40.8 52.1 %collective-permute-start.15 = (f32[32,5120]{1,0:T(8,128)}, f32[32,5120]{1,0:T(8,128)}, u32[]{:S(2)}, u32[]{:S(2)}) collective-permute-start(f32[32,5120]{1,0:T(8,128)} %get-tuple-element.140.refs_0_), channel_id=1, source_target_pairs={{0,1},{1,0},{2,3},{3,2},{4,5},{5,4},{6,7},{7,6},{8,9},{9,8},{10,11... | collective-permute-start | bytes 1966088 | tf_op jit(solution)/shard_map/ppermute | solution.py:78
  58.3 30.9 %collective-permute-start.10 = (f32[128,1280]{1,0:T(8,128)}, f32[128,1280]{1,0:T(8,128)S(1)}, u32[]{:S(2)}, u32[]{:S(2)}) collective-permute-start(f32[128,1280]{1,0:T(8,128)} %get-tuple-element.78), channel_id=1, source_target_pairs={{0,8},{8,0},{16,24},{24,16},{1,9},{9,1},{17,25},{25,17},{2,10},{10... | collective-permute-start | bytes 1966088 | tf_op jit(solution)/shard_map/ppermute | solution.py:78
  68.6 20.6 %copy-start.30 = (f32[32,5120]{1,0:T(8,128)}, f32[32,5120]{1,0:T(8,128)S(1)}, u32[]{:S(2)}) copy-start(f32[32,5120]{1,0:T(8,128)S(1)} %collective-permute-done.8.refs_4_) | copy-start | bytes 1966084
  68.6 20.6 %copy-start.32 = (f32[32,5120]{1,0:T(8,128)}, f32[32,5120]{1,0:T(8,128)S(1)}, u32[]{:S(2)}) copy-start(f32[32,5120]{1,0:T(8,128)S(1)} %collective-permute-done.9.refs_6_) | copy-start | bytes 1966084
  68.6 20.6 %collective-permute-start.12 = (f32[32,5120]{1,0:T(8,128)S(1)}, f32[32,5120]{1,0:T(8,128)S(1)}, u32[]{:S(2)}, u32[]{:S(2)}) collective-permute-start(f32[32,5120]{1,0:T(8,128)S(1)} %collective-permute-done.8.refs_4_), channel_id=1, source_target_pairs={{0,1},{1,0},{2,3},{3,2},{4,5},{5,4},{6,7},{7,6},{8,9},{9,8},{10,11... | collective-permute-start | bytes 1966088 | tf_op jit(solution)/shard_map/ppermute | solution.py:78
  68.7 20.5 %collective-permute-start.13 = (f32[32,5120]{1,0:T(8,128)S(1)}, f32[32,5120]{1,0:T(8,128)S(1)}, u32[]{:S(2)}, u32[]{:S(2)}) collective-permute-start(f32[32,5120]{1,0:T(8,128)S(1)} %collective-permute-done.9.refs_6_), channel_id=1, source_target_pairs={{0,1},{1,0},{2,3},{3,2},{4,5},{5,4},{6,7},{7,6},{8,9},{9,8},{10,11... | collective-permute-start | bytes 1966088 | tf_op jit(solution)/shard_map/ppermute | solution.py:78
  71.7 21.2 %copy-start.21 = (f32[2560]{0:T(1024)}, f32[2560]{0:T(1024)S(1)}, u32[]{:S(2)}) copy-start(f32[2560]{0:T(1024)S(1)} %add.92) | copy-start | bytes 30724
  71.7 17.7 %copy-start.15 = (f32[32,5120]{1,0:T(8,128)S(1)}, f32[32,5120]{1,0:T(8,128)}, u32[]{:S(2)}) copy-start(f32[32,5120]{1,0:T(8,128)} %get-tuple-element.140.refs_0_) | copy-start | bytes 1966084
  71.7 21.2 %copy-start.18 = (f32[128,1280]{1,0:T(8,128)S(1)}, f32[128,1280]{1,0:T(8,128)}, u32[]{:S(2)}) copy-start(f32[128,1280]{1,0:T(8,128)} %get-tuple-element.77) | copy-start | bytes 1966084
  89.2 8.0 %copy-start.33 = (f32[32,5120]{1,0:T(8,128)}, f32[32,5120]{1,0:T(8,128)S(1)}, u32[]{:S(2)}) copy-start(f32[32,5120]{1,0:T(8,128)S(1)} %collective-permute-done.12.refs_5_) | copy-start | bytes 1966084
  89.3 5.3 %collective-permute-start.20 = (f32[32,5120]{1,0:T(8,128)}, f32[32,5120]{1,0:T(8,128)}, u32[]{:S(2)}, u32[]{:S(2)}) collective-permute-start(f32[32,5120]{1,0:T(8,128)} %collective-permute-done.11.refs_2_), channel_id=1, source_target_pairs={{0,1},{1,0},{2,3},{3,2},{4,5},{5,4},{6,7},{7,6},{8,9},{9,8},{10,11... | collective-permute-start | bytes 1966088 | tf_op jit(solution)/shard_map/ppermute | solution.py:78
  89.4 37.3 %collective-permute-start.16 = (f32[32,5120]{1,0:T(8,128)S(1)}, f32[32,5120]{1,0:T(8,128)S(1)}, u32[]{:S(2)}, u32[]{:S(2)}) collective-permute-start(f32[32,5120]{1,0:T(8,128)S(1)} %copy-done.15), channel_id=1, source_target_pairs={{0,2},{1,3},{2,0},{3,1},{4,6},{5,7},{6,4},{7,5},{8,10},{9,11},{10,... | collective-permute-start | bytes 1966088 | tf_op jit(solution)/shard_map/ppermute | solution.py:78
  90.1 37.4 %collective-permute-start.17 = (f32[32,5120]{1,0:T(8,128)S(1)}, f32[32,5120]{1,0:T(8,128)}, u32[]{:S(2)}, u32[]{:S(2)}) collective-permute-start(f32[32,5120]{1,0:T(8,128)S(1)} %copy-done.15), channel_id=1, source_target_pairs={{0,4},{1,5},{2,6},{3,7},{4,0},{5,1},{6,2},{7,3},{8,12},{9,13},{10,... | collective-permute-start | bytes 1966088 | tf_op jit(solution)/shard_map/ppermute | solution.py:78
  91.5 36.8 %collective-permute-start.18 = (f32[32,5120]{1,0:T(8,128)S(1)}, f32[32,5120]{1,0:T(8,128)}, u32[]{:S(2)}, u32[]{:S(2)}) collective-permute-start(f32[32,5120]{1,0:T(8,128)S(1)} %copy-done.15), channel_id=1, source_target_pairs={{0,6},{1,7},{2,4},{3,5},{4,2},{5,3},{6,0},{7,1},{8,14},{9,15},{10,... | collective-permute-start | bytes 1966088 | tf_op jit(solution)/shard_map/ppermute | solution.py:78
  93.0 35.3 %collective-permute-start.14 = (f32[128,1280]{1,0:T(8,128)}, f32[128,1280]{1,0:T(8,128)S(1)}, u32[]{:S(2)}, u32[]{:S(2)}) collective-permute-start(f32[128,1280]{1,0:T(8,128)} %get-tuple-element.87), channel_id=1, source_target_pairs={{0,8},{8,0},{16,24},{24,16},{1,9},{9,1},{17,25},{25,17},{2,10},{10... | collective-permute-start | bytes 1966088 | tf_op jit(solution)/shard_map/ppermute | solution.py:78
  94.6 33.7 %collective-permute-start.19 = (f32[64,1280]{1,0:T(8,128)S(1)}, f32[64,1280]{1,0:T(8,128)S(1)}, u32[]{:S(2)}, u32[]{:S(2)}) collective-permute-start(f32[64,1280]{1,0:T(8,128)S(1)} %slice_add_fusion.6), channel_id=1, source_target_pairs={{0,16},{8,24},{16,0},{24,8},{1,17},{9,25},{17,1},{25,9},{2,18},{10... | collective-permute-start | bytes 983048 | tf_op jit(solution)/shard_map/ppermute | solution.py:78
  126.7 2.8 %collective-permute-start.22 = (f32[32,5120]{1,0:T(8,128)S(1)}, f32[32,5120]{1,0:T(8,128)S(1)}, u32[]{:S(2)}, u32[]{:S(2)}) collective-permute-start(f32[32,5120]{1,0:T(8,128)S(1)} %get-tuple-element.137.refs_0_), channel_id=1, source_target_pairs={{0,1},{1,0},{2,3},{3,2},{4,5},{5,4},{6,7},{7,6},{8,9},{9,8},{10,11... | collective-permute-start | bytes 1966088 | tf_op jit(solution)/shard_map/ppermute | solution.py:78
  127.6 37.1 %collective-permute-start.23 = (f32[32,5120]{1,0:T(8,128)S(1)}, f32[32,5120]{1,0:T(8,128)S(1)}, u32[]{:S(2)}, u32[]{:S(2)}) collective-permute-start(f32[32,5120]{1,0:T(8,128)S(1)} %get-tuple-element.137.refs_0_), channel_id=1, source_target_pairs={{0,2},{1,3},{2,0},{3,1},{4,6},{5,7},{6,4},{7,5},{8,10},{9,11},{10,... | collective-permute-start | bytes 1966088 | tf_op jit(solution)/shard_map/ppermute | solution.py:78
  128.4 2.6 collective-permute-start.27
  128.4 4.8 %collective-permute-start.28 = (f32[32,5120]{1,0:T(8,128)}, f32[32,5120]{1,0:T(8,128)S(1)}, u32[]{:S(2)}, u32[]{:S(2)}) collective-permute-start(f32[32,5120]{1,0:T(8,128)} %collective-permute-done.17.refs_4_), channel_id=1, source_target_pairs={{0,1},{1,0},{2,3},{3,2},{4,5},{5,4},{6,7},{7,6},{8,9},{9,8},{10,11... | collective-permute-start | bytes 1966088 | tf_op jit(solution)/shard_map/ppermute | solution.py:78
  128.9 5.2 %collective-permute-start.29 = (f32[32,5120]{1,0:T(8,128)}, f32[32,5120]{1,0:T(8,128)S(1)}, u32[]{:S(2)}, u32[]{:S(2)}) collective-permute-start(f32[32,5120]{1,0:T(8,128)} %collective-permute-done.18.refs_6_), channel_id=1, source_target_pairs={{0,1},{1,0},{2,3},{3,2},{4,5},{5,4},{6,7},{7,6},{8,9},{9,8},{10,11... | collective-permute-start | bytes 1966088 | tf_op jit(solution)/shard_map/ppermute | solution.py:78
  129.5 42.8 %copy-start.13 = (f32[128,2560]{1,0:T(8,128)S(1)}, f32[128,2560]{1,0:T(8,128)}, u32[]{:S(2)}) copy-start(f32[128,2560]{1,0:T(8,128)} %get-tuple-element.94) | copy-start | bytes 3932164
  129.5 35.2 %copy-start.2 = (f32[32,5120]{1,0:T(8,128)}, f32[32,5120]{1,0:T(8,128)S(1)}, u32[]{:S(2)}) copy-start(f32[32,5120]{1,0:T(8,128)S(1)} %collective-permute-done.22.refs_1_) | copy-start | bytes 1966084
  129.5 36.5 %collective-permute-start.24 = (f32[32,5120]{1,0:T(8,128)S(1)}, f32[32,5120]{1,0:T(8,128)S(1)}, u32[]{:S(2)}, u32[]{:S(2)}) collective-permute-start(f32[32,5120]{1,0:T(8,128)S(1)} %get-tuple-element.137.refs_0_), channel_id=1, source_target_pairs={{0,4},{1,5},{2,6},{3,7},{4,0},{5,1},{6,2},{7,3},{8,12},{9,13},{10,... | collective-permute-start | bytes 1966088 | tf_op jit(solution)/shard_map/ppermute | solution.py:78
  131.0 35.0 %collective-permute-start.25 = (f32[32,5120]{1,0:T(8,128)S(1)}, f32[32,5120]{1,0:T(8,128)S(1)}, u32[]{:S(2)}, u32[]{:S(2)}) collective-permute-start(f32[32,5120]{1,0:T(8,128)S(1)} %get-tuple-element.137.refs_0_), channel_id=1, source_target_pairs={{0,6},{1,7},{2,4},{3,5},{4,2},{5,3},{6,0},{7,1},{8,14},{9,15},{10,... | collective-permute-start | bytes 1966088 | tf_op jit(solution)/shard_map/ppermute | solution.py:78
  133.3 39.1 %collective-permute-start.21 = (f32[128,2560]{1,0:T(8,128)}, f32[128,2560]{1,0:T(8,128)}, u32[]{:S(2)}, u32[]{:S(2)}) collective-permute-start(f32[128,2560]{1,0:T(8,128)} %get-tuple-element.95), channel_id=1, source_target_pairs={{0,8},{8,0},{16,24},{24,16},{1,9},{9,1},{17,25},{25,17},{2,10},{10... | collective-permute-start | bytes 3932168 | tf_op jit(solution)/shard_map/ppermute | solution.py:78
  135.0 35.2 %collective-permute-start.26 = (f32[64,1280]{1,0:T(8,128)S(1)}, f32[64,1280]{1,0:T(8,128)S(1)}, u32[]{:S(2)}, u32[]{:S(2)}) collective-permute-start(f32[64,1280]{1,0:T(8,128)S(1)} %slice_add_fusion.5), channel_id=1, source_target_pairs={{0,16},{8,24},{16,0},{24,8},{1,17},{9,25},{17,1},{25,9},{2,18},{10... | collective-permute-start | bytes 983048 | tf_op jit(solution)/shard_map/ppermute | solution.py:78
  164.7 11.3 %copy-start.22 = (f32[2560]{0:T(1024)S(1)}, f32[2560]{0:T(1024)}, u32[]{:S(2)}) copy-start(f32[2560]{0:T(1024)} %copy-done.21) | copy-start | bytes 30724
  164.7 13.7 %copy-start.3 = (f32[32,5120]{1,0:T(8,128)}, f32[32,5120]{1,0:T(8,128)S(1)}, u32[]{:S(2)}) copy-start(f32[32,5120]{1,0:T(8,128)S(1)} %collective-permute-done.23.refs_2_) | copy-start | bytes 1966084
  164.7 49.7 %collective-permute-start.30 = (f32[128,2560]{1,0:T(8,128)}, f32[128,2560]{1,0:T(8,128)}, u32[]{:S(2)}, u32[]{:S(2)}) collective-permute-start(f32[128,2560]{1,0:T(8,128)} %get-tuple-element.107), channel_id=1, source_target_pairs={{0,8},{8,0},{16,24},{24,16},{1,9},{9,1},{17,25},{25,17},{2,10},{10... | collective-permute-start | bytes 3932168 | tf_op jit(solution)/shard_map/ppermute | solution.py:78
  166.0 12.4 %copy-start.5 = (f32[32,5120]{1,0:T(8,128)}, f32[32,5120]{1,0:T(8,128)S(1)}, u32[]{:S(2)}) copy-start(f32[32,5120]{1,0:T(8,128)S(1)} %collective-permute-done.24.refs_4_) | copy-start | bytes 1966084
  166.0 12.4 %copy-start.8 = (f32[32,5120]{1,0:T(8,128)}, f32[32,5120]{1,0:T(8,128)S(1)}, u32[]{:S(2)}) copy-start(f32[32,5120]{1,0:T(8,128)S(1)} %collective-permute-done.25.refs_6_) | copy-start | bytes 1966084
  174.4 3.9 %collective-permute-start.32 = (f32[32,5120]{1,0:T(8,128)S(1)}, f32[32,5120]{1,0:T(8,128)S(1)}, u32[]{:S(2)}, u32[]{:S(2)}) collective-permute-start(f32[32,5120]{1,0:T(8,128)S(1)} %collective-permute-done.23.refs_2_), channel_id=1, source_target_pairs={{0,1},{1,0},{2,3},{3,2},{4,5},{5,4},{6,7},{7,6},{8,9},{9,8},{10,11... | collective-permute-start | bytes 1966088 | tf_op jit(solution)/shard_map/ppermute | solution.py:78
  174.4 3.9 %collective-permute-start.33 = (f32[32,5120]{1,0:T(8,128)S(1)}, f32[32,5120]{1,0:T(8,128)S(1)}, u32[]{:S(2)}, u32[]{:S(2)}) collective-permute-start(f32[32,5120]{1,0:T(8,128)S(1)} %collective-permute-done.24.refs_4_), channel_id=1, source_target_pairs={{0,1},{1,0},{2,3},{3,2},{4,5},{5,4},{6,7},{7,6},{8,9},{9,8},{10,11... | collective-permute-start | bytes 1966088 | tf_op jit(solution)/shard_map/ppermute | solution.py:78
  174.9 3.5 %collective-permute-start.34 = (f32[32,5120]{1,0:T(8,128)S(1)}, f32[32,5120]{1,0:T(8,128)S(1)}, u32[]{:S(2)}, u32[]{:S(2)}) collective-permute-start(f32[32,5120]{1,0:T(8,128)S(1)} %collective-permute-done.25.refs_6_), channel_id=1, source_target_pairs={{0,1},{1,0},{2,3},{3,2},{4,5},{5,4},{6,7},{7,6},{8,9},{9,8},{10,11... | collective-permute-start | bytes 1966088 | tf_op jit(solution)/shard_map/ppermute | solution.py:78
  176.1 38.4 %collective-permute-start.31 = (f32[64,2560]{1,0:T(8,128)}, f32[64,2560]{1,0:T(8,128)S(1)}, u32[]{:S(2)}, u32[]{:S(2)}) collective-permute-start(f32[64,2560]{1,0:T(8,128)} %slice_add_fusion.1), channel_id=1, source_target_pairs={{0,16},{8,24},{16,0},{24,8},{1,17},{9,25},{17,1},{25,9},{2,18},{10... | collective-permute-start | bytes 1966088 | tf_op jit(solution)/shard_map/ppermute | solution.py:78
  197.6 18.1 %copy-start.14 = (f32[128,2560]{1,0:T(8,128)S(1)}, f32[128,2560]{1,0:T(8,128)}, u32[]{:S(2)}) copy-start(f32[128,2560]{1,0:T(8,128)} %get-tuple-element.106) | copy-start | bytes 3932164
  197.6 39.0 %collective-permute-start.35 = (f32[128,1280]{1,0:T(8,128)}, f32[128,1280]{1,0:T(8,128)S(1)}, u32[]{:S(2)}, u32[]{:S(2)}) collective-permute-start(f32[128,1280]{1,0:T(8,128)} %get-tuple-element.119), channel_id=1, source_target_pairs={{0,8},{8,0},{16,24},{24,16},{1,9},{9,1},{17,25},{25,17},{2,10},{10... | collective-permute-start | bytes 1966088 | tf_op jit(solution)/shard_map/ppermute | solution.py:78
  216.9 29.7 %copy-start.19 = (f32[128,1280]{1,0:T(8,128)S(1)}, f32[128,1280]{1,0:T(8,128)}, u32[]{:S(2)}) copy-start(f32[128,1280]{1,0:T(8,128)} %get-tuple-element.118) | copy-start | bytes 1966084
  216.9 29.7 %collective-permute-start.36 = (f32[64,2560]{1,0:T(8,128)S(1)}, f32[64,2560]{1,0:T(8,128)S(1)}, u32[]{:S(2)}, u32[]{:S(2)}) collective-permute-start(f32[64,2560]{1,0:T(8,128)S(1)} %slice_add_fusion), channel_id=1, source_target_pairs={{0,16},{8,24},{16,0},{24,8},{1,17},{9,25},{17,1},{25,9},{2,18},{10... | collective-permute-start | bytes 1966088 | tf_op jit(solution)/shard_map/ppermute | solution.py:78
  235.6 26.8 %copy-start.20 = (f32[128,1280]{1,0:T(8,128)S(1)}, f32[128,1280]{1,0:T(8,128)}, u32[]{:S(2)}) copy-start(f32[128,1280]{1,0:T(8,128)} %get-tuple-element.126) | copy-start | bytes 1966084
  235.6 26.8 %collective-permute-start.38 = (f32[128,1280]{1,0:T(8,128)}, f32[128,1280]{1,0:T(8,128)S(1)}, u32[]{:S(2)}, u32[]{:S(2)}) collective-permute-start(f32[128,1280]{1,0:T(8,128)} %get-tuple-element.127), channel_id=1, source_target_pairs={{0,8},{8,0},{16,24},{24,16},{1,9},{9,1},{17,25},{25,17},{2,10},{10... | collective-permute-start | bytes 1966088 | tf_op jit(solution)/shard_map/ppermute | solution.py:78
  246.7 16.8 %collective-permute-start.37 = (f32[64,1280]{1,0:T(8,128)S(1)}, f32[64,1280]{1,0:T(8,128)S(1)}, u32[]{:S(2)}, u32[]{:S(2)}) collective-permute-start(f32[64,1280]{1,0:T(8,128)S(1)} %slice_add_fusion.4), channel_id=1, source_target_pairs={{0,16},{8,24},{16,0},{24,8},{1,17},{9,25},{17,1},{25,9},{2,18},{10... | collective-permute-start | bytes 983048 | tf_op jit(solution)/shard_map/ppermute | solution.py:78
  262.4 13.8 %collective-permute-start.39 = (f32[64,1280]{1,0:T(8,128)S(1)}, f32[64,1280]{1,0:T(8,128)S(1)}, u32[]{:S(2)}, u32[]{:S(2)}) collective-permute-start(f32[64,1280]{1,0:T(8,128)S(1)} %slice_add_fusion.2), channel_id=1, source_target_pairs={{0,16},{8,24},{16,0},{24,8},{1,17},{9,25},{17,1},{25,9},{2,18},{10... | collective-permute-start | bytes 983048 | tf_op jit(solution)/shard_map/ppermute | solution.py:78
  (14 other events, 37.5 us)

commit v2 on v1

--- a/solution.py
+++ b/solution.py
@@ -7,7 +7,7 @@
 from jax.experimental.pallas import tpu as pltpu
 from jax.sharding import PartitionSpec as P
 
-PLAN = ((1, (1, 1)), (1, (1,)), (1, (1,)), (1, (1, 1)))
+PLAN = ((1, (1,)), (1, (1,)), (1, (1,)), (1, (1, 1)))
 TILE_BYTES = 5500000
 
 
@@ -179,47 +179,43 @@
         for turn in range(rounds):
             ladder = ladder + held["sum", p, turn][:block]
         denom = vir_sum[None, None, offset : offset + width] - occ_sum[:, first:last, None]
-        written.add(p)
         return lax.dynamic_update_slice(update, ladder.reshape(group, last - first, width) / denom, (0, first, offset))
 
-    made, written = {}, set()
+    made = {}
     held[0, 0] = amplitudes[parts[0][0] : parts[0][1]]
     gather(0, evens[1:], 0)
+    if len(evens) > 1:
+        held[0, evens[-1]], later = lax.optimization_barrier(
+            (held[0, evens[-1]], (amplitudes, vir_first, vir_second, occ_first, occ_second))
+        )
+        amplitudes, vir_first, vir_second, occ_first, occ_second = later
+    for number, part in enumerate(parts[1:], 1):
+        steps.post((number, 0), amplitudes[part[0] : part[1]], 0)
+    occ_sum = (lookup(occ_energy, occ_first) + lookup(occ_energy, occ_second)).reshape(group, own)
+    vir_sum = lookup(vir_energy, vir_first) + lookup(vir_energy, vir_second)
+    steps.post("terms", (occ_sum, vir_sum), 0)
     gather(0, [q + 1 for q in evens], 0)
-    terms_at = min(1, count - 1)
     for step in range(count + 1):
-        if step == terms_at:
-            steps.post("terms", (vir_first, vir_second, occ_first, occ_second), step)
+        if step < count:
+            number, piece, pieces, first, last, offset, width = todo[step]
+            if number + 1 < len(parts) and step:
+                steps.post((number + 1, 0), held[number + 1, 0], step)
         place = steps.settle(step, place)
-        if step == terms_at:
-            vir_first, vir_second, occ_first, occ_second = held["terms"]
-            occ_sum = (lookup(occ_energy, occ_first) + lookup(occ_energy, occ_second)).reshape(group, own)
-            vir_sum = lookup(vir_energy, vir_first) + lookup(vir_energy, vir_second)
-            steps.post("denominators", (occ_sum, vir_sum, jnp.zeros((group, own, columns), jnp.float32)), step + 1)
-        if step > terms_at:
-            occ_sum, vir_sum, update = held["denominators"]
         if step == count:
             break
-        number, piece, pieces, first, last, offset, width = todo[step]
         m = last - first
         block = group * m
         if number + 1 < len(parts):
-            if piece == 0:
-                held[number + 1, 0] = amplitudes[parts[number + 1][0] : parts[number + 1][1]]
-                gather(number + 1, [1], step + 1)
-            cut = [evens[1:][(col_size // 2 - 1) * k // pieces : (col_size // 2 - 1) * (k + 1) // pieces] for k in range(pieces)][::-1]
+            cut = [evens[1:][-(-(col_size // 2 - 1) * k // pieces) : -(-(col_size // 2 - 1) * (k + 1) // pieces)] for k in range(pieces)]
             gather(number + 1, cut[piece], step + 1)
             if piece:
-                gather(number + 1, [q + 1 for q in cut[piece - 1]], step + 1)
+                gather(number + 1, [q + 1 for q in ([0] if piece == 1 else []) + cut[piece - 1]], step + 1)
         if piece == 0 and number:
             gather(number, [q + 1 for q in evens if (number, q + 1) not in held], step)
         for p in range(step):
             turn = step - 1 - p
             if 0 < turn < rounds:
                 steps.post(("sum", p, turn), send(p, turn), step + 1)
-            if turn == rounds and step > terms_at:
-                update = write(update, p)
-                steps.post("denominators", (occ_sum, vir_sum, update), step + 1)
         sources = [held[number, q] for q in range(col_size)]
         cuts = [(0, size // 2 * block), (size // 2 * block, size * block)] if size > 1 else [(0, block)]
         made[step] = product(place, sources, m, integrals, offset, width, cuts)
@@ -230,9 +226,10 @@
         for p in range(count):
             if ("sum", p, turn) not in held:
                 held["sum", p, turn] = send(p, turn)
+    occ_sum, vir_sum = held["terms"]
+    update = jnp.zeros((group, own, columns), jnp.float32)
     for p in range(count):
-        if p not in written:
-            update = write(update, p)
+        update = write(update, p)
     return update.reshape(group * own, columns)
 
 

time: 279 us -> 268 us (0.961)
  waiting for transfers between devices: 96.7 us -> 87.4 us
  Pallas kernels: 128 us -> 123 us
  starting transfers between devices: 29.5 us -> 32.6 us
    ppermute x40 -> x38, waiting for transfers between devices: 96.7 us -> 87.4 us  [across(): return lax.ppermute(block, axis, [(i, i ^ bits) for i in range(size)])]
    pallas_call x6 -> x5, Pallas kernels: 128 us -> 123 us  [product(): pl.pallas_call(functools.partial(product_kernel, m, len(sources), cuts),...]
    ppermute x40 -> x38, starting transfers between devices: 29.5 us -> 32.6 us  [across(): return lax.ppermute(block, axis, [(i, i ^ bits) for i in range(size)])]
  transfers between devices with their start and end apart: 40 -> 38, of which waited for: 9 -> 10; matrix products, arithmetic and copies ran while one was open for 5% -> 6% of each run, Pallas kernels for 46% -> 46%
where the time goes in v2:
time: 268 us; the launch traced here: 266 us
  Pallas kernels  123 us (46%)
  waiting for transfers between devices  87.4 us (33%)
  starting transfers between devices  32.6 us (12%)
  other arithmetic  14.6 us (5%)
  local copies, waits for them, and re-layouts  7.65 us (3%)
    pallas_call x5, Pallas kernels, product(): pl.pallas_call(functools.partial(product_kernel, m, len(sources), cuts),...  123 us
    ppermute x38, waiting for transfers between devices, across(): return lax.ppermute(block, axis, [(i, i ^ bits) for i in range(size)])  87.4 us
    ppermute x38, starting transfers between devices, across(): return lax.ppermute(block, axis, [(i, i ^ bits) for i in range(size)])  32.6 us
  transfers between devices with their start and end apart: 38, of which 10 were waited for; matrix products, arithmetic and copies ran while one was open for 6% of the time, Pallas kernels for 46%

profile of v2, /device:TPU:0, one launch (start us, length us, event | category | flops | bytes accessed | tf_op | source)
XLA Modules:
  0.0 265.8 jit_solution(10833158289607917072)
XLA Ops:
  0.0 1.2 slice.91.refs_0_
  1.2 4.0 %collective-permute-start.2 = (f32[32,5120]{1,0:T(8,128)S(1)}, f32[32,5120]{1,0:T(8,128)S(1)}, u32[]{:S(2)}, u32[]{:S(2)}) collective-permute-start(f32[32,5120]{1,0:T(8,128)S(1)} %slice.91.refs_0_), channel_id=1, source_target_pairs={{0,6},{1,7},{2,4},{3,5},{4,2},{5,3},{6,0},{7,1},{8,14},{9,15},{10,... | collective-permute-start | bytes 1966088 | tf_op jit(solution)/shard_map/ppermute | solution.py:78
  5.2 0.5 collective-permute-start.1
  5.7 0.1 collective-permute-start
  5.8 0.6 fusion.2.place_ref
  6.4 14.4 %collective-permute-done.2.refs_6_ = f32[32,5120]{1,0:T(8,128)S(1)} collective-permute-done((f32[32,5120]{1,0:T(8,128)S(1)}, f32[32,5120]{1,0:T(8,128)S(1)}, u32[]{:S(2)}, u32[]{:S(2)}) %collective-permute-start.2) | collective-permute-done | bytes 655392 | tf_op jit(solution)/shard_map/ppermute | solution.py:78
  20.8 13.2 %collective-permute-done.1.refs_4_ = f32[32,5120]{1,0:T(8,128)S(1)} collective-permute-done((f32[32,5120]{1,0:T(8,128)S(1)}, f32[32,5120]{1,0:T(8,128)S(1)}, u32[]{:S(2)}, u32[]{:S(2)}) %collective-permute-start.1) | collective-permute-done | bytes 655392 | tf_op jit(solution)/shard_map/ppermute | solution.py:78
  34.0 0.1 collective-permute-start.5
  34.1 0.3 collective-permute-done.refs_2_
  34.4 0.1 collective-permute-start.4
  34.5 1.6 fusion.6
  36.2 2.3 select_reduce_fusion
  38.7 0.5 collective-permute-start.14
  39.1 1.5 collective-permute-start.9
  40.7 1.4 collective-permute-start.8
  42.1 0.5 collective-permute-start.7
  42.7 29.4 %ladder_product.5 = (f32[128,2560]{1,0:T(8,128)}, f32[128,2560]{1,0:T(8,128)}) custom-call(s32[8]{0:T(128)} %fusion.2.place_ref, f32[32,5120]{1,0:T(8,128)} %copy-done.11, f32[32,5120]{1,0:T(8,128)} %collective-permute-done.3.refs_1_, f32[32,5120]{1,0:T(8,128)} %collective-permute-done.refs_2_, f32[32,5120]{1,0:T(8,128)} %copy-done.28, ...), custom_call_target="tpu_custom_call" | custom-call | flops 20132659200 | bytes 60293120 | tf_op jit(solution)/shard_map/ladder_product/pallas_call | solution.py:60
  72.2 0.5 collective-permute-start.16
  72.8 1.6 collective-permute-start.10
  74.5 0.2 collective-permute-start.23
  74.7 1.6 collective-permute-start.13
  76.3 1.3 collective-permute-start.12
  77.7 0.5 collective-permute-start.11
  78.2 29.4 %ladder_product.6 = (f32[128,2560]{1,0:T(8,128)}, f32[128,2560]{1,0:T(8,128)}) custom-call(s32[8]{0:T(128)} %fusion.2.place_ref, f32[32,5120]{1,0:T(8,128)} %copy-done.15, f32[32,5120]{1,0:T(8,128)} %collective-permute-done.14.refs_1_, f32[32,5120]{1,0:T(8,128)} %collective-permute-done.7.refs_2_, f32[32,5120]{1,0:T(8,128)} %copy-done.29, ...), custom_call_target="tpu_custom_call" | custom-call | flops 20132659200 | bytes 60293120 | tf_op jit(solution)/shard_map/ladder_product/pallas_call | solution.py:60
  107.6 2.4 collective-permute-start.18
  110.1 0.5 collective-permute-start.25
  110.8 1.4 collective-permute-start.21
  112.2 0.3 collective-permute-done.24.refs_3_
  112.6 0.7 collective-permute-start.20
  113.3 0.7 collective-permute-done.25.refs_5_
  113.9 0.7 collective-permute-start.19
  114.7 0.1 copy-done.31
  114.8 0.9 copy-done.32
  115.7 2.6 collective-permute-start.22
  118.3 29.5 %ladder_product.7 = (f32[128,2560]{1,0:T(8,128)}, f32[128,2560]{1,0:T(8,128)}) custom-call(s32[8]{0:T(128)} %fusion.2.place_ref, f32[32,5120]{1,0:T(8,128)} %copy-done.14, f32[32,5120]{1,0:T(8,128)} %copy-done.24, f32[32,5120]{1,0:T(8,128)} %collective-permute-done.11.refs_2_, f32[32,5120]{1,0:T(8,128)} %copy-done.30, f32[32,5120]{1,0:T(8,128)} %copy-done.25, ...), custom_call_target="tpu_custom_call" | custom-call | flops 20132659200 | bytes 60293120 | tf_op jit(solution)/shard_map/ladder_product/pallas_call | solution.py:60
  147.8 4.5 %collective-permute-done.22 = f32[64,2560]{1,0:T(8,128)} collective-permute-done((f32[64,2560]{1,0:T(8,128)S(1)}, f32[64,2560]{1,0:T(8,128)}, u32[]{:S(2)}, u32[]{:S(2)}) %collective-permute-start.22) | collective-permute-done | bytes 655392 | tf_op jit(solution)/shard_map/ppermute | solution.py:78
  152.4 3.5 %collective-permute-start.27 = (f32[128,2560]{1,0:T(8,128)}, f32[128,2560]{1,0:T(8,128)}, u32[]{:S(2)}, u32[]{:S(2)}) collective-permute-start(f32[128,2560]{1,0:T(8,128)} %get-tuple-element.89), channel_id=1, source_target_pairs={{0,8},{8,0},{16,24},{24,16},{1,9},{9,1},{17,25},{25,17},{2,10},{10... | collective-permute-start | bytes 3932168 | tf_op jit(solution)/shard_map/ppermute | solution.py:78
  155.9 1.7 add_add_fusion.2
  157.6 0.2 collective-permute-start.30
  157.8 0.3 collective-permute-start.31
  158.2 0.2 collective-permute-start.32
  158.3 0.2 subtract_divide_fusion
  158.5 1.8 dynamic_update_slice.15
  160.3 2.0 slice_add_fusion.1
  162.3 0.4 collective-permute-start.28
  162.7 0.4 copy-done.4
  163.1 0.4 copy-done.5
  163.5 0.2 copy-done.6
  163.7 0.8 copy-done.7
  164.6 17.3 %ladder_product.8 = (f32[128,1280]{1,0:T(8,128)}, f32[128,1280]{1,0:T(8,128)}) custom-call(s32[8]{0:T(128)} %fusion.2.place_ref, f32[32,5120]{1,0:T(8,128)} %copy-done, f32[32,5120]{1,0:T(8,128)} %copy-done.4, f32[32,5120]{1,0:T(8,128)} %copy-done.3, f32[32,5120]{1,0:T(8,128)} %copy-done.5, f32[32,5120]{1,0:T(8,128)} %copy-done.2, f32[32,5120]{1,0:T(8,128)} %copy-done.6, ...), custom_call_target="tpu_custom_call" | custom-call | flops 10066329600 | bytes 32768000 | tf_op jit(solution)/shard_map/ladder_product/pallas_call | solution.py:60
  181.9 1.8 collective-permute-start.33
  183.7 16.2 %collective-permute-done.27 = f32[128,2560]{1,0:T(8,128)} collective-permute-done((f32[128,2560]{1,0:T(8,128)}, f32[128,2560]{1,0:T(8,128)}, u32[]{:S(2)}, u32[]{:S(2)}) %collective-permute-start.27) | collective-permute-done | bytes 1310752 | tf_op jit(solution)/shard_map/ppermute | solution.py:78
  199.9 1.4 add_add_fusion.1
  201.3 1.2 slice_add_fusion
  202.5 2.8 %collective-permute-start.34 = (f32[64,2560]{1,0:T(8,128)S(1)}, f32[64,2560]{1,0:T(8,128)S(1)}, u32[]{:S(2)}, u32[]{:S(2)}) collective-permute-start(f32[64,2560]{1,0:T(8,128)S(1)} %slice_add_fusion), channel_id=1, source_target_pairs={{0,16},{8,24},{16,0},{24,8},{1,17},{9,25},{17,1},{25,9},{2,18},{10... | collective-permute-start | bytes 1966088 | tf_op jit(solution)/shard_map/ppermute | solution.py:78
  205.3 17.4 %ladder_product.9 = (f32[128,1280]{1,0:T(8,128)}, f32[128,1280]{1,0:T(8,128)}) custom-call(s32[8]{0:T(128)} %fusion.2.place_ref, f32[32,5120]{1,0:T(8,128)} %copy-done, f32[32,5120]{1,0:T(8,128)} %copy-done.4, f32[32,5120]{1,0:T(8,128)} %copy-done.3, f32[32,5120]{1,0:T(8,128)} %copy-done.5, f32[32,5120]{1,0:T(8,128)} %copy-done.2, f32[32,5120]{1,0:T(8,128)} %copy-done.6, ...), custom_call_target="tpu_custom_call" | custom-call | flops 10066329600 | bytes 32768000 | tf_op jit(solution)/shard_map/ladder_product/pallas_call | solution.py:60
  222.8 1.0 divide_dynamic-update-slice_fusion.1
  223.8 10.1 %collective-permute-done.34 = f32[64,2560]{1,0:T(8,128)S(1)} collective-permute-done((f32[64,2560]{1,0:T(8,128)S(1)}, f32[64,2560]{1,0:T(8,128)S(1)}, u32[]{:S(2)}, u32[]{:S(2)}) %collective-permute-start.34) | collective-permute-done | bytes 655392 | tf_op jit(solution)/shard_map/ppermute | solution.py:78
  234.0 1.2 add_add_fusion
  235.2 15.2 %collective-permute-done.36 = f32[128,1280]{1,0:T(8,128)S(1)} collective-permute-done((f32[128,1280]{1,0:T(8,128)}, f32[128,1280]{1,0:T(8,128)S(1)}, u32[]{:S(2)}, u32[]{:S(2)}) %collective-permute-start.36) | collective-permute-done | bytes 655392 | tf_op jit(solution)/shard_map/ppermute | solution.py:78
  250.5 1.0 divide_dynamic-update-slice_fusion
  251.6 0.8 divide_dynamic-update-slice_fusion.3
  252.4 12.5 %collective-permute-done.37 = f32[64,1280]{1,0:T(8,128)S(1)} collective-permute-done((f32[64,1280]{1,0:T(8,128)S(1)}, f32[64,1280]{1,0:T(8,128)S(1)}, u32[]{:S(2)}, u32[]{:S(2)}) %collective-permute-start.37) | collective-permute-done | bytes 327712 | tf_op jit(solution)/shard_map/ppermute | solution.py:78
  265.0 0.8 divide_dynamic-update-slice_fusion.2
  (108 shorter events, 1.2 us)
Async XLA Ops:
  0.0 36.1 %copy-start.16 = (s32[2560]{0:T(1024)S(1)}, s32[2560]{0:T(1024)}, u32[]{:S(2)}) copy-start(s32[2560]{0:T(1024)} %param.15) | copy-start | bytes 30724
  0.0 36.1 %copy-start.17 = (s32[2560]{0:T(1024)S(1)}, s32[2560]{0:T(1024)}, u32[]{:S(2)}) copy-start(s32[2560]{0:T(1024)} %param.14) | copy-start | bytes 30724
  0.0 38.5 %copy-start.19 = (s32[256]{0:T(256)S(1)}, s32[256]{0:T(256)}, u32[]{:S(2)}) copy-start(s32[256]{0:T(256)} %param.13) | copy-start | bytes 3076
  0.0 38.5 %copy-start.20 = (s32[256]{0:T(256)S(1)}, s32[256]{0:T(256)}, u32[]{:S(2)}) copy-start(s32[256]{0:T(256)} %param.12) | copy-start | bytes 3076
  0.0 36.1 %copy-start.18 = (f32[256]{0:T(256)S(1)}, f32[256]{0:T(256)}, u32[]{:S(2)}) copy-start(f32[256]{0:T(256)} %param.11) | copy-start | bytes 3076
  0.0 38.5 %copy-start.21 = (f32[64]{0:T(128)S(1)}, f32[64]{0:T(128)}, u32[]{:S(2)}) copy-start(f32[64]{0:T(128)} %param.10) | copy-start | bytes 772
  1.2 41.4 %copy-start.11 = (f32[32,5120]{1,0:T(8,128)}, f32[32,5120]{1,0:T(8,128)S(1)}, u32[]{:S(2)}) copy-start(f32[32,5120]{1,0:T(8,128)S(1)} %slice.91.refs_0_) | copy-start | bytes 1966084
  1.2 19.6 %collective-permute-start.2 = (f32[32,5120]{1,0:T(8,128)S(1)}, f32[32,5120]{1,0:T(8,128)S(1)}, u32[]{:S(2)}, u32[]{:S(2)}) collective-permute-start(f32[32,5120]{1,0:T(8,128)S(1)} %slice.91.refs_0_), channel_id=1, source_target_pairs={{0,6},{1,7},{2,4},{3,5},{4,2},{5,3},{6,0},{7,1},{8,14},{9,15},{10,... | collective-permute-start | bytes 1966088 | tf_op jit(solution)/shard_map/ppermute | solution.py:78
  5.2 28.8 %collective-permute-start.1 = (f32[32,5120]{1,0:T(8,128)S(1)}, f32[32,5120]{1,0:T(8,128)S(1)}, u32[]{:S(2)}, u32[]{:S(2)}) collective-permute-start(f32[32,5120]{1,0:T(8,128)S(1)} %slice.91.refs_0_), channel_id=1, source_target_pairs={{0,4},{1,5},{2,6},{3,7},{4,0},{5,1},{6,2},{7,3},{8,12},{9,13},{10,... | collective-permute-start | bytes 1966088 | tf_op jit(solution)/shard_map/ppermute | solution.py:78
  5.7 28.7 %collective-permute-start = (f32[32,5120]{1,0:T(8,128)S(1)}, f32[32,5120]{1,0:T(8,128)}, u32[]{:S(2)}, u32[]{:S(2)}) collective-permute-start(f32[32,5120]{1,0:T(8,128)S(1)} %slice.91.refs_0_), channel_id=1, source_target_pairs={{0,2},{1,3},{2,0},{3,1},{4,6},{5,7},{6,4},{7,5},{8,10},{9,11},{10,... | collective-permute-start | bytes 1966088 | tf_op jit(solution)/shard_map/ppermute | solution.py:78
  5.8 32.8 %collective-permute-start.3 = (f32[32,5120]{1,0:T(8,128)S(1)}, f32[32,5120]{1,0:T(8,128)}, u32[]{:S(2)}, u32[]{:S(2)}) collective-permute-start(f32[32,5120]{1,0:T(8,128)S(1)} %slice.91.refs_0_), channel_id=1, source_target_pairs={{0,1},{1,0},{2,3},{3,2},{4,5},{5,4},{6,7},{7,6},{8,9},{9,8},{10,11... | collective-permute-start | bytes 1966088 | tf_op jit(solution)/shard_map/ppermute | solution.py:78
  20.8 21.9 %copy-start.22 = (f32[32,5120]{1,0:T(8,128)}, f32[32,5120]{1,0:T(8,128)S(1)}, u32[]{:S(2)}) copy-start(f32[32,5120]{1,0:T(8,128)S(1)} %collective-permute-done.2.refs_6_) | copy-start | bytes 1966084
  20.8 17.8 %collective-permute-start.6 = (f32[32,5120]{1,0:T(8,128)S(1)}, f32[32,5120]{1,0:T(8,128)S(1)}, u32[]{:S(2)}, u32[]{:S(2)}) collective-permute-start(f32[32,5120]{1,0:T(8,128)S(1)} %collective-permute-done.2.refs_6_), channel_id=1, source_target_pairs={{0,1},{1,0},{2,3},{3,2},{4,5},{5,4},{6,7},{7,6},{8,9},{9,8},{10,11... | collective-permute-start | bytes 1966088 | tf_op jit(solution)/shard_map/ppermute | solution.py:78
  34.0 8.7 %copy-start.23 = (f32[32,5120]{1,0:T(8,128)}, f32[32,5120]{1,0:T(8,128)S(1)}, u32[]{:S(2)}) copy-start(f32[32,5120]{1,0:T(8,128)S(1)} %collective-permute-done.1.refs_4_) | copy-start | bytes 1966084
  34.0 4.7 %collective-permute-start.5 = (f32[32,5120]{1,0:T(8,128)S(1)}, f32[32,5120]{1,0:T(8,128)S(1)}, u32[]{:S(2)}, u32[]{:S(2)}) collective-permute-start(f32[32,5120]{1,0:T(8,128)S(1)} %collective-permute-done.1.refs_4_), channel_id=1, source_target_pairs={{0,1},{1,0},{2,3},{3,2},{4,5},{5,4},{6,7},{7,6},{8,9},{9,8},{10,11... | collective-permute-start | bytes 1966088 | tf_op jit(solution)/shard_map/ppermute | solution.py:78
  34.4 4.3 %collective-permute-start.4 = (f32[32,5120]{1,0:T(8,128)}, f32[32,5120]{1,0:T(8,128)S(1)}, u32[]{:S(2)}, u32[]{:S(2)}) collective-permute-start(f32[32,5120]{1,0:T(8,128)} %collective-permute-done.refs_2_), channel_id=1, source_target_pairs={{0,1},{1,0},{2,3},{3,2},{4,5},{5,4},{6,7},{7,6},{8,9},{9,8},{10,11... | collective-permute-start | bytes 1966088 | tf_op jit(solution)/shard_map/ppermute | solution.py:78
  36.1 36.0 %copy-start.15 = (f32[32,5120]{1,0:T(8,128)}, f32[32,5120]{1,0:T(8,128)S(1)}, u32[]{:S(2)}) copy-start(f32[32,5120]{1,0:T(8,128)S(1)} %get-tuple-element.71.refs_0_) | copy-start | bytes 1966084
  36.1 41.5 %copy-start.14 = (f32[32,5120]{1,0:T(8,128)}, f32[32,5120]{1,0:T(8,128)S(1)}, u32[]{:S(2)}) copy-start(f32[32,5120]{1,0:T(8,128)S(1)} %get-tuple-element.75.refs_0_) | copy-start | bytes 1966084
  36.1 116.2 %copy-start = (f32[32,5120]{1,0:T(8,128)}, f32[32,5120]{1,0:T(8,128)S(1)}, u32[]{:S(2)}) copy-start(f32[32,5120]{1,0:T(8,128)S(1)} %get-tuple-element.84.refs_0_) | copy-start | bytes 1966084
  38.6 4.0 %copy-start.26 = (f32[32,5120]{1,0:T(8,128)}, f32[32,5120]{1,0:T(8,128)S(1)}, u32[]{:S(2)}) copy-start(f32[32,5120]{1,0:T(8,128)S(1)} %collective-permute-done.6.refs_7_) | copy-start | bytes 1966084
  38.7 4.0 %copy-start.27 = (f32[32,5120]{1,0:T(8,128)}, f32[32,5120]{1,0:T(8,128)S(1)}, u32[]{:S(2)}) copy-start(f32[32,5120]{1,0:T(8,128)S(1)} %collective-permute-done.5.refs_5_) | copy-start | bytes 1966084
  38.7 2.0 copy-start.28
  38.7 35.8 %collective-permute-start.14 = (f32[32,5120]{1,0:T(8,128)S(1)}, f32[32,5120]{1,0:T(8,128)}, u32[]{:S(2)}, u32[]{:S(2)}) collective-permute-start(f32[32,5120]{1,0:T(8,128)S(1)} %get-tuple-element.71.refs_0_), channel_id=1, source_target_pairs={{0,1},{1,0},{2,3},{3,2},{4,5},{5,4},{6,7},{7,6},{8,9},{9,8},{10,11... | collective-permute-start | bytes 1966088 | tf_op jit(solution)/shard_map/ppermute | solution.py:78
  39.1 33.0 %collective-permute-start.9 = (f32[32,5120]{1,0:T(8,128)S(1)}, f32[32,5120]{1,0:T(8,128)}, u32[]{:S(2)}, u32[]{:S(2)}) collective-permute-start(f32[32,5120]{1,0:T(8,128)S(1)} %get-tuple-element.71.refs_0_), channel_id=1, source_target_pairs={{0,6},{1,7},{2,4},{3,5},{4,2},{5,3},{6,0},{7,1},{8,14},{9,15},{10,... | collective-permute-start | bytes 1966088 | tf_op jit(solution)/shard_map/ppermute | solution.py:78
  40.7 31.5 %collective-permute-start.8 = (f32[32,5120]{1,0:T(8,128)S(1)}, f32[32,5120]{1,0:T(8,128)}, u32[]{:S(2)}, u32[]{:S(2)}) collective-permute-start(f32[32,5120]{1,0:T(8,128)S(1)} %get-tuple-element.71.refs_0_), channel_id=1, source_target_pairs={{0,4},{1,5},{2,6},{3,7},{4,0},{5,1},{6,2},{7,3},{8,12},{9,13},{10,... | collective-permute-start | bytes 1966088 | tf_op jit(solution)/shard_map/ppermute | solution.py:78
  42.1 30.0 %collective-permute-start.7 = (f32[32,5120]{1,0:T(8,128)S(1)}, f32[32,5120]{1,0:T(8,128)}, u32[]{:S(2)}, u32[]{:S(2)}) collective-permute-start(f32[32,5120]{1,0:T(8,128)S(1)} %get-tuple-element.71.refs_0_), channel_id=1, source_target_pairs={{0,2},{1,3},{2,0},{3,1},{4,6},{5,7},{6,4},{7,5},{8,10},{9,11},{10,... | collective-permute-start | bytes 1966088 | tf_op jit(solution)/shard_map/ppermute | solution.py:78
  72.1 2.6 collective-permute-start.15
  72.2 4.1 %collective-permute-start.16 = (f32[32,5120]{1,0:T(8,128)}, f32[32,5120]{1,0:T(8,128)}, u32[]{:S(2)}, u32[]{:S(2)}) collective-permute-start(f32[32,5120]{1,0:T(8,128)} %collective-permute-done.8.refs_4_), channel_id=1, source_target_pairs={{0,1},{1,0},{2,3},{3,2},{4,5},{5,4},{6,7},{7,6},{8,9},{9,8},{10,11... | collective-permute-start | bytes 1966088 | tf_op jit(solution)/shard_map/ppermute | solution.py:78
  72.7 4.9 %collective-permute-start.17 = (f32[32,5120]{1,0:T(8,128)}, f32[32,5120]{1,0:T(8,128)}, u32[]{:S(2)}, u32[]{:S(2)}) collective-permute-start(f32[32,5120]{1,0:T(8,128)} %collective-permute-done.9.refs_6_), channel_id=1, source_target_pairs={{0,1},{1,0},{2,3},{3,2},{4,5},{5,4},{6,7},{7,6},{8,9},{9,8},{10,11... | collective-permute-start | bytes 1966088 | tf_op jit(solution)/shard_map/ppermute | solution.py:78
  72.8 37.3 %collective-permute-start.10 = (f32[128,2560]{1,0:T(8,128)}, f32[128,2560]{1,0:T(8,128)S(1)}, u32[]{:S(2)}, u32[]{:S(2)}) collective-permute-start(f32[128,2560]{1,0:T(8,128)} %get-tuple-element.72), channel_id=1, source_target_pairs={{0,8},{8,0},{16,24},{24,16},{1,9},{9,1},{17,25},{25,17},{2,10},{10... | collective-permute-start | bytes 3932168 | tf_op jit(solution)/shard_map/ppermute | solution.py:78
  74.5 36.3 %copy-start.8 = (f32[128,2560]{1,0:T(8,128)S(1)}, f32[128,2560]{1,0:T(8,128)}, u32[]{:S(2)}) copy-start(f32[128,2560]{1,0:T(8,128)} %get-tuple-element.70) | copy-start | bytes 3932164
  74.5 36.3 %collective-permute-start.23 = (f32[32,5120]{1,0:T(8,128)S(1)}, f32[32,5120]{1,0:T(8,128)S(1)}, u32[]{:S(2)}, u32[]{:S(2)}) collective-permute-start(f32[32,5120]{1,0:T(8,128)S(1)} %get-tuple-element.75.refs_0_), channel_id=1, source_target_pairs={{0,1},{1,0},{2,3},{3,2},{4,5},{5,4},{6,7},{7,6},{8,9},{9,8},{10,11... | collective-permute-start | bytes 1966088 | tf_op jit(solution)/shard_map/ppermute | solution.py:78
  74.7 3.5 %copy-start.29 = (f32[32,5120]{1,0:T(8,128)}, f32[32,5120]{1,0:T(8,128)S(1)}, u32[]{:S(2)}) copy-start(f32[32,5120]{1,0:T(8,128)S(1)} %collective-permute-done.15.refs_3_) | copy-start | bytes 1966084
  74.7 32.9 %collective-permute-start.13 = (f32[32,5120]{1,0:T(8,128)S(1)}, f32[32,5120]{1,0:T(8,128)}, u32[]{:S(2)}, u32[]{:S(2)}) collective-permute-start(f32[32,5120]{1,0:T(8,128)S(1)} %get-tuple-element.75.refs_0_), channel_id=1, source_target_pairs={{0,6},{1,7},{2,4},{3,5},{4,2},{5,3},{6,0},{7,1},{8,14},{9,15},{10,... | collective-permute-start | bytes 1966088 | tf_op jit(solution)/shard_map/ppermute | solution.py:78
  76.3 33.7 %collective-permute-start.12 = (f32[32,5120]{1,0:T(8,128)S(1)}, f32[32,5120]{1,0:T(8,128)S(1)}, u32[]{:S(2)}, u32[]{:S(2)}) collective-permute-start(f32[32,5120]{1,0:T(8,128)S(1)} %get-tuple-element.75.refs_0_), channel_id=1, source_target_pairs={{0,4},{1,5},{2,6},{3,7},{4,0},{5,1},{6,2},{7,3},{8,12},{9,13},{10,... | collective-permute-start | bytes 1966088 | tf_op jit(solution)/shard_map/ppermute | solution.py:78
  77.7 32.4 %collective-permute-start.11 = (f32[32,5120]{1,0:T(8,128)S(1)}, f32[32,5120]{1,0:T(8,128)}, u32[]{:S(2)}, u32[]{:S(2)}) collective-permute-start(f32[32,5120]{1,0:T(8,128)S(1)} %get-tuple-element.75.refs_0_), channel_id=1, source_target_pairs={{0,2},{1,3},{2,0},{3,1},{4,6},{5,7},{6,4},{7,5},{8,10},{9,11},{10,... | collective-permute-start | bytes 1966088 | tf_op jit(solution)/shard_map/ppermute | solution.py:78
  107.6 48.3 %collective-permute-start.18 = (f32[128,2560]{1,0:T(8,128)}, f32[128,2560]{1,0:T(8,128)}, u32[]{:S(2)}, u32[]{:S(2)}) collective-permute-start(f32[128,2560]{1,0:T(8,128)} %get-tuple-element.80), channel_id=1, source_target_pairs={{0,8},{8,0},{16,24},{24,16},{1,9},{9,1},{17,25},{25,17},{2,10},{10... | collective-permute-start | bytes 3932168 | tf_op jit(solution)/shard_map/ppermute | solution.py:78
  110.0 3.2 %copy-start.25 = (f32[32,5120]{1,0:T(8,128)}, f32[32,5120]{1,0:T(8,128)S(1)}, u32[]{:S(2)}) copy-start(f32[32,5120]{1,0:T(8,128)S(1)} %collective-permute-done.12.refs_4_) | copy-start | bytes 1966084
  110.1 2.5 collective-permute-start.24
  110.1 3.8 %collective-permute-start.25 = (f32[32,5120]{1,0:T(8,128)S(1)}, f32[32,5120]{1,0:T(8,128)S(1)}, u32[]{:S(2)}, u32[]{:S(2)}) collective-permute-start(f32[32,5120]{1,0:T(8,128)S(1)} %collective-permute-done.12.refs_4_), channel_id=1, source_target_pairs={{0,1},{1,0},{2,3},{3,2},{4,5},{5,4},{6,7},{7,6},{8,9},{9,8},{10,11... | collective-permute-start | bytes 1966088 | tf_op jit(solution)/shard_map/ppermute | solution.py:78
  110.6 4.0 %collective-permute-start.26 = (f32[32,5120]{1,0:T(8,128)}, f32[32,5120]{1,0:T(8,128)S(1)}, u32[]{:S(2)}, u32[]{:S(2)}) collective-permute-start(f32[32,5120]{1,0:T(8,128)} %collective-permute-done.13.refs_6_), channel_id=1, source_target_pairs={{0,1},{1,0},{2,3},{3,2},{4,5},{5,4},{6,7},{7,6},{8,9},{9,8},{10,11... | collective-permute-start | bytes 1966088 | tf_op jit(solution)/shard_map/ppermute | solution.py:78
  110.8 41.6 %collective-permute-start.21 = (f32[32,5120]{1,0:T(8,128)S(1)}, f32[32,5120]{1,0:T(8,128)S(1)}, u32[]{:S(2)}, u32[]{:S(2)}) collective-permute-start(f32[32,5120]{1,0:T(8,128)S(1)} %get-tuple-element.84.refs_0_), channel_id=1, source_target_pairs={{0,6},{1,7},{2,4},{3,5},{4,2},{5,3},{6,0},{7,1},{8,14},{9,15},{10,... | collective-permute-start | bytes 1966088 | tf_op jit(solution)/shard_map/ppermute | solution.py:78
  112.6 2.1 copy-start.30
  112.6 43.3 %collective-permute-start.20 = (f32[32,5120]{1,0:T(8,128)S(1)}, f32[32,5120]{1,0:T(8,128)S(1)}, u32[]{:S(2)}, u32[]{:S(2)}) collective-permute-start(f32[32,5120]{1,0:T(8,128)S(1)} %get-tuple-element.84.refs_0_), channel_id=1, source_target_pairs={{0,4},{1,5},{2,6},{3,7},{4,0},{5,1},{6,2},{7,3},{8,12},{9,13},{10,... | collective-permute-start | bytes 1966088 | tf_op jit(solution)/shard_map/ppermute | solution.py:78
  113.9 41.9 %collective-permute-start.19 = (f32[32,5120]{1,0:T(8,128)S(1)}, f32[32,5120]{1,0:T(8,128)S(1)}, u32[]{:S(2)}, u32[]{:S(2)}) collective-permute-start(f32[32,5120]{1,0:T(8,128)S(1)} %get-tuple-element.84.refs_0_), channel_id=1, source_target_pairs={{0,2},{1,3},{2,0},{3,1},{4,6},{5,7},{6,4},{7,5},{8,10},{9,11},{10,... | collective-permute-start | bytes 1966088 | tf_op jit(solution)/shard_map/ppermute | solution.py:78
  115.7 36.7 %collective-permute-start.22 = (f32[64,2560]{1,0:T(8,128)S(1)}, f32[64,2560]{1,0:T(8,128)}, u32[]{:S(2)}, u32[]{:S(2)}) collective-permute-start(f32[64,2560]{1,0:T(8,128)S(1)} %slice_add_fusion.2), channel_id=1, source_target_pairs={{0,16},{8,24},{16,0},{24,8},{1,17},{9,25},{17,1},{25,9},{2,18},{10... | collective-permute-start | bytes 1966088 | tf_op jit(solution)/shard_map/ppermute | solution.py:78
  152.4 10.0 %collective-permute-start.29 = (f32[32,5120]{1,0:T(8,128)S(1)}, f32[32,5120]{1,0:T(8,128)S(1)}, u32[]{:S(2)}, u32[]{:S(2)}) collective-permute-start(f32[32,5120]{1,0:T(8,128)S(1)} %get-tuple-element.84.refs_0_), channel_id=1, source_target_pairs={{0,1},{1,0},{2,3},{3,2},{4,5},{5,4},{6,7},{7,6},{8,9},{9,8},{10,11... | collective-permute-start | bytes 1966088 | tf_op jit(solution)/shard_map/ppermute | solution.py:78
  152.4 7.9 %copy-start.1 = (f32[32,5120]{1,0:T(8,128)}, f32[32,5120]{1,0:T(8,128)S(1)}, u32[]{:S(2)}) copy-start(f32[32,5120]{1,0:T(8,128)S(1)} %collective-permute-done.21.refs_6_) | copy-start | bytes 1966084
  152.4 47.5 %collective-permute-start.27 = (f32[128,2560]{1,0:T(8,128)}, f32[128,2560]{1,0:T(8,128)}, u32[]{:S(2)}, u32[]{:S(2)}) collective-permute-start(f32[128,2560]{1,0:T(8,128)} %get-tuple-element.89), channel_id=1, source_target_pairs={{0,8},{8,0},{16,24},{24,16},{1,9},{9,1},{17,25},{25,17},{2,10},{10... | collective-permute-start | bytes 3932168 | tf_op jit(solution)/shard_map/ppermute | solution.py:78
  155.9 4.4 %copy-start.2 = (f32[32,5120]{1,0:T(8,128)}, f32[32,5120]{1,0:T(8,128)S(1)}, u32[]{:S(2)}) copy-start(f32[32,5120]{1,0:T(8,128)S(1)} %collective-permute-done.20.refs_4_) | copy-start | bytes 1966084
  155.9 4.4 %copy-start.3 = (f32[32,5120]{1,0:T(8,128)}, f32[32,5120]{1,0:T(8,128)S(1)}, u32[]{:S(2)}) copy-start(f32[32,5120]{1,0:T(8,128)S(1)} %collective-permute-done.19.refs_2_) | copy-start | bytes 1966084
  157.6 2.7 %copy-start.9 = (f32[128,2560]{1,0:T(8,128)S(1)}, f32[128,2560]{1,0:T(8,128)}, u32[]{:S(2)}) copy-start(f32[128,2560]{1,0:T(8,128)} %get-tuple-element.79) | copy-start | bytes 3932164
  157.6 5.1 %collective-permute-start.30 = (f32[32,5120]{1,0:T(8,128)S(1)}, f32[32,5120]{1,0:T(8,128)S(1)}, u32[]{:S(2)}, u32[]{:S(2)}) collective-permute-start(f32[32,5120]{1,0:T(8,128)S(1)} %collective-permute-done.19.refs_2_), channel_id=1, source_target_pairs={{0,1},{1,0},{2,3},{3,2},{4,5},{5,4},{6,7},{7,6},{8,9},{9,8},{10,11... | collective-permute-start | bytes 1966088 | tf_op jit(solution)/shard_map/ppermute | solution.py:78
  157.8 4.8 %collective-permute-start.31 = (f32[32,5120]{1,0:T(8,128)S(1)}, f32[32,5120]{1,0:T(8,128)S(1)}, u32[]{:S(2)}, u32[]{:S(2)}) collective-permute-start(f32[32,5120]{1,0:T(8,128)S(1)} %collective-permute-done.20.refs_4_), channel_id=1, source_target_pairs={{0,1},{1,0},{2,3},{3,2},{4,5},{5,4},{6,7},{7,6},{8,9},{9,8},{10,11... | collective-permute-start | bytes 1966088 | tf_op jit(solution)/shard_map/ppermute | solution.py:78
  158.2 4.5 %collective-permute-start.32 = (f32[32,5120]{1,0:T(8,128)S(1)}, f32[32,5120]{1,0:T(8,128)S(1)}, u32[]{:S(2)}, u32[]{:S(2)}) collective-permute-start(f32[32,5120]{1,0:T(8,128)S(1)} %collective-permute-done.21.refs_6_), channel_id=1, source_target_pairs={{0,1},{1,0},{2,3},{3,2},{4,5},{5,4},{6,7},{7,6},{8,9},{9,8},{10,11... | collective-permute-start | bytes 1966088 | tf_op jit(solution)/shard_map/ppermute | solution.py:78
  162.3 37.6 %collective-permute-start.28 = (f32[64,2560]{1,0:T(8,128)}, f32[64,2560]{1,0:T(8,128)S(1)}, u32[]{:S(2)}, u32[]{:S(2)}) collective-permute-start(f32[64,2560]{1,0:T(8,128)} %slice_add_fusion.1), channel_id=1, source_target_pairs={{0,16},{8,24},{16,0},{24,8},{1,17},{9,25},{17,1},{25,9},{2,18},{10... | collective-permute-start | bytes 1966088 | tf_op jit(solution)/shard_map/ppermute | solution.py:78
  181.9 19.4 %copy-start.10 = (f32[128,2560]{1,0:T(8,128)S(1)}, f32[128,2560]{1,0:T(8,128)}, u32[]{:S(2)}) copy-start(f32[128,2560]{1,0:T(8,128)} %get-tuple-element.88) | copy-start | bytes 3932164
  181.9 41.8 %collective-permute-start.33 = (f32[128,1280]{1,0:T(8,128)}, f32[128,1280]{1,0:T(8,128)S(1)}, u32[]{:S(2)}, u32[]{:S(2)}) collective-permute-start(f32[128,1280]{1,0:T(8,128)} %get-tuple-element.99), channel_id=1, source_target_pairs={{0,8},{8,0},{16,24},{24,16},{1,9},{9,1},{17,25},{25,17},{2,10},{10... | collective-permute-start | bytes 1966088 | tf_op jit(solution)/shard_map/ppermute | solution.py:78
  202.5 31.4 %copy-start.12 = (f32[128,1280]{1,0:T(8,128)S(1)}, f32[128,1280]{1,0:T(8,128)}, u32[]{:S(2)}) copy-start(f32[128,1280]{1,0:T(8,128)} %get-tuple-element.98) | copy-start | bytes 1966084
  202.5 31.4 %collective-permute-start.34 = (f32[64,2560]{1,0:T(8,128)S(1)}, f32[64,2560]{1,0:T(8,128)S(1)}, u32[]{:S(2)}, u32[]{:S(2)}) collective-permute-start(f32[64,2560]{1,0:T(8,128)S(1)} %slice_add_fusion), channel_id=1, source_target_pairs={{0,16},{8,24},{16,0},{24,8},{1,17},{9,25},{17,1},{25,9},{2,18},{10... | collective-permute-start | bytes 1966088 | tf_op jit(solution)/shard_map/ppermute | solution.py:78
  222.7 27.7 %copy-start.13 = (f32[128,1280]{1,0:T(8,128)S(1)}, f32[128,1280]{1,0:T(8,128)}, u32[]{:S(2)}) copy-start(f32[128,1280]{1,0:T(8,128)} %get-tuple-element.103) | copy-start | bytes 1966084
  222.7 27.7 %collective-permute-start.36 = (f32[128,1280]{1,0:T(8,128)}, f32[128,1280]{1,0:T(8,128)S(1)}, u32[]{:S(2)}, u32[]{:S(2)}) collective-permute-start(f32[128,1280]{1,0:T(8,128)} %get-tuple-element.104), channel_id=1, source_target_pairs={{0,8},{8,0},{16,24},{24,16},{1,9},{9,1},{17,25},{25,17},{2,10},{10... | collective-permute-start | bytes 1966088 | tf_op jit(solution)/shard_map/ppermute | solution.py:78
  233.9 17.6 %collective-permute-start.35 = (f32[64,1280]{1,0:T(8,128)S(1)}, f32[64,1280]{1,0:T(8,128)S(1)}, u32[]{:S(2)}, u32[]{:S(2)}) collective-permute-start(f32[64,1280]{1,0:T(8,128)S(1)} %slice_add_fusion.5), channel_id=1, source_target_pairs={{0,16},{8,24},{16,0},{24,8},{1,17},{9,25},{17,1},{25,9},{2,18},{10... | collective-permute-start | bytes 983048 | tf_op jit(solution)/shard_map/ppermute | solution.py:78
  250.4 14.5 %collective-permute-start.37 = (f32[64,1280]{1,0:T(8,128)S(1)}, f32[64,1280]{1,0:T(8,128)S(1)}, u32[]{:S(2)}, u32[]{:S(2)}) collective-permute-start(f32[64,1280]{1,0:T(8,128)S(1)} %slice_add_fusion.3), channel_id=1, source_target_pairs={{0,16},{8,24},{16,0},{24,8},{1,17},{9,25},{17,1},{25,9},{2,18},{10... | collective-permute-start | bytes 983048 | tf_op jit(solution)/shard_map/ppermute | solution.py:78
  (7 other events, 6.8 us)

commit v3 on v2

--- a/solution.py
+++ b/solution.py
@@ -186,28 +186,34 @@
     gather(0, evens[1:], 0)
     if len(evens) > 1:
         held[0, evens[-1]], later = lax.optimization_barrier(
-            (held[0, evens[-1]], (amplitudes, vir_first, vir_second, occ_first, occ_second))
+            (held[0, evens[-1]], amplitudes)
         )
-        amplitudes, vir_first, vir_second, occ_first, occ_second = later
+        amplitudes = later
     for number, part in enumerate(parts[1:], 1):
         steps.post((number, 0), amplitudes[part[0] : part[1]], 0)
-    occ_sum = (lookup(occ_energy, occ_first) + lookup(occ_energy, occ_second)).reshape(group, own)
-    vir_sum = lookup(vir_energy, vir_first) + lookup(vir_energy, vir_second)
-    steps.post("terms", (occ_sum, vir_sum), 0)
+    steps.post("indices", (vir_first, vir_second, occ_first, occ_second), 1)
     gather(0, [q + 1 for q in evens], 0)
+    if len(parts) > 1:
+        gather(1, evens[1:], 1)
     for step in range(count + 1):
         if step < count:
             number, piece, pieces, first, last, offset, width = todo[step]
             if number + 1 < len(parts) and step:
                 steps.post((number + 1, 0), held[number + 1, 0], step)
         place = steps.settle(step, place)
+        if step == 1:
+            vir_first, vir_second, occ_first, occ_second = held["indices"]
+            occ_sum = (lookup(occ_energy, occ_first) + lookup(occ_energy, occ_second)).reshape(group, own)
+            vir_sum = lookup(vir_energy, vir_first) + lookup(vir_energy, vir_second)
+            steps.post("terms", (occ_sum, vir_sum), 2)
         if step == count:
             break
         m = last - first
         block = group * m
         if number + 1 < len(parts):
             cut = [evens[1:][-(-(col_size // 2 - 1) * k // pieces) : -(-(col_size // 2 - 1) * (k + 1) // pieces)] for k in range(pieces)]
-            gather(number + 1, cut[piece], step + 1)
+            if step:
+                gather(number + 1, cut[piece], step + 1)
             if piece:
                 gather(number + 1, [q + 1 for q in ([0] if piece == 1 else []) + cut[piece - 1]], step + 1)
         if piece == 0 and number:

time: 268 us -> 267 us (level)
  transfers between devices with their start and end apart: 38 -> 38, of which waited for: 10 -> 9; matrix products, arithmetic and copies ran while one was open for 6% -> 7% of each run, Pallas kernels for 46% -> 46%
where the time goes in v3:
time: 267 us; the launch traced here: 265 us
  Pallas kernels  123 us (46%)
  waiting for transfers between devices  86.7 us (32%)
  starting transfers between devices  30.3 us (11%)
  other arithmetic  15.5 us (6%)
  local copies, waits for them, and re-layouts  8.8 us (3%)
    pallas_call x5, Pallas kernels, product(): pl.pallas_call(functools.partial(product_kernel, m, len(sources), cuts),...  123 us
    ppermute x38, waiting for transfers between devices, across(): return lax.ppermute(block, axis, [(i, i ^ bits) for i in range(size)])  86.7 us
    ppermute x38, starting transfers between devices, across(): return lax.ppermute(block, axis, [(i, i ^ bits) for i in range(size)])  30.3 us
  transfers between devices with their start and end apart: 38, of which 9 were waited for; matrix products, arithmetic and copies ran while one was open for 7% of the time, Pallas kernels for 46%

profile of v3, /device:TPU:0, one launch (start us, length us, event | category | flops | bytes accessed | tf_op | source)
XLA Modules:
  0.0 264.8 jit_solution(18267018801567442113)
XLA Ops:
  0.0 1.1 slice.91.refs_0_
  1.1 4.0 %collective-permute-start.2 = (f32[32,5120]{1,0:T(8,128)S(1)}, f32[32,5120]{1,0:T(8,128)S(1)}, u32[]{:S(2)}, u32[]{:S(2)}) collective-permute-start(f32[32,5120]{1,0:T(8,128)S(1)} %slice.91.refs_0_), channel_id=1, source_target_pairs={{0,6},{1,7},{2,4},{3,5},{4,2},{5,3},{6,0},{7,1},{8,14},{9,15},{10,... | collective-permute-start | bytes 1966088 | tf_op jit(solution)/shard_map/ppermute | solution.py:78
  5.1 0.5 collective-permute-start.1
  5.6 0.1 collective-permute-start
  5.8 0.6 fusion.2.place_ref
  6.4 14.3 %collective-permute-done.2.refs_6_ = f32[32,5120]{1,0:T(8,128)S(1)} collective-permute-done((f32[32,5120]{1,0:T(8,128)S(1)}, f32[32,5120]{1,0:T(8,128)S(1)}, u32[]{:S(2)}, u32[]{:S(2)}) %collective-permute-start.2) | collective-permute-done | bytes 655392 | tf_op jit(solution)/shard_map/ppermute | solution.py:78
  20.7 13.2 %collective-permute-done.1.refs_4_ = f32[32,5120]{1,0:T(8,128)S(1)} collective-permute-done((f32[32,5120]{1,0:T(8,128)S(1)}, f32[32,5120]{1,0:T(8,128)S(1)}, u32[]{:S(2)}, u32[]{:S(2)}) %collective-permute-start.1) | collective-permute-done | bytes 655392 | tf_op jit(solution)/shard_map/ppermute | solution.py:78
  33.9 0.1 collective-permute-start.5
  34.0 0.3 collective-permute-done.refs_2_
  34.3 0.1 collective-permute-start.4
  34.4 1.6 fusion.6
  36.0 1.9 collective-permute-start.9
  37.9 1.3 collective-permute-start.8
  39.3 0.4 collective-permute-start.7
  39.7 0.9 copy-done.31
  40.7 29.4 %ladder_product.5 = (f32[128,2560]{1,0:T(8,128)}, f32[128,2560]{1,0:T(8,128)}) custom-call(s32[8]{0:T(128)} %fusion.2.place_ref, f32[32,5120]{1,0:T(8,128)} %copy-done.11, f32[32,5120]{1,0:T(8,128)} %collective-permute-done.3.refs_1_, f32[32,5120]{1,0:T(8,128)} %collective-permute-done.refs_2_, f32[32,5120]{1,0:T(8,128)} %copy-done.31, ...), custom_call_target="tpu_custom_call" | custom-call | flops 20132659200 | bytes 60293120 | tf_op jit(solution)/shard_map/ladder_product/pallas_call | solution.py:60
  70.1 0.5 collective-permute-start.15
  70.7 0.4 collective-permute-start.17
  71.3 2.3 select_reduce_fusion
  73.6 0.1 select_reduce_fusion.2
  73.8 1.9 collective-permute-start.13
  75.6 1.3 collective-permute-start.12
  76.9 0.4 collective-permute-start.11
  77.4 0.4 copy-done.27
  77.8 0.9 copy-done.28
  78.7 1.6 collective-permute-start.10
  80.3 29.4 %ladder_product.6 = (f32[128,2560]{1,0:T(8,128)}, f32[128,2560]{1,0:T(8,128)}) custom-call(s32[8]{0:T(128)} %fusion.2.place_ref, f32[32,5120]{1,0:T(8,128)} %copy-done.15, f32[32,5120]{1,0:T(8,128)} %collective-permute-done.14.refs_1_, f32[32,5120]{1,0:T(8,128)} %collective-permute-done.7.refs_2_, f32[32,5120]{1,0:T(8,128)} %copy-done.26, ...), custom_call_target="tpu_custom_call" | custom-call | flops 20132659200 | bytes 60293120 | tf_op jit(solution)/shard_map/ladder_product/pallas_call | solution.py:60
  109.7 0.5 collective-permute-start.18
  110.4 0.5 collective-permute-start.25
  110.9 0.9 slice_add_fusion.2
  111.9 1.5 collective-permute-start.21
  113.4 1.2 collective-permute-start.20
  114.6 0.8 collective-permute-start.19
  115.4 2.6 collective-permute-start.22
  117.9 29.5 %ladder_product.7 = (f32[128,2560]{1,0:T(8,128)}, f32[128,2560]{1,0:T(8,128)}) custom-call(s32[8]{0:T(128)} %fusion.2.place_ref, f32[32,5120]{1,0:T(8,128)} %copy-done.14, f32[32,5120]{1,0:T(8,128)} %copy-done.22, f32[32,5120]{1,0:T(8,128)} %collective-permute-done.11.refs_2_, f32[32,5120]{1,0:T(8,128)} %collective-permute-done.24.refs_3_, ...), custom_call_target="tpu_custom_call" | custom-call | flops 20132659200 | bytes 60293120 | tf_op jit(solution)/shard_map/ladder_product/pallas_call | solution.py:60
  147.4 7.0 %collective-permute-done.18 = f32[128,2560]{1,0:T(8,128)} collective-permute-done((f32[128,2560]{1,0:T(8,128)}, f32[128,2560]{1,0:T(8,128)}, u32[]{:S(2)}, u32[]{:S(2)}) %collective-permute-start.18) | collective-permute-done | bytes 1310752 | tf_op jit(solution)/shard_map/ppermute | solution.py:78
  154.5 2.6 collective-permute-start.27
  157.1 1.7 add_add_fusion.2
  158.9 0.5 collective-permute-start.31
  159.5 0.2 subtract_divide_fusion
  159.6 1.8 dynamic_update_slice.15
  161.4 2.0 slice_add_fusion.1
  163.4 0.6 collective-permute-start.28
  164.0 0.2 copy-done.4
  164.3 0.6 copy-done.5
  164.9 0.2 copy-done.6
  165.1 0.9 copy-done.7
  165.9 17.4 %ladder_product.8 = (f32[128,1280]{1,0:T(8,128)}, f32[128,1280]{1,0:T(8,128)}) custom-call(s32[8]{0:T(128)} %fusion.2.place_ref, f32[32,5120]{1,0:T(8,128)} %copy-done, f32[32,5120]{1,0:T(8,128)} %copy-done.4, f32[32,5120]{1,0:T(8,128)} %copy-done.3, f32[32,5120]{1,0:T(8,128)} %copy-done.5, f32[32,5120]{1,0:T(8,128)} %copy-done.2, f32[32,5120]{1,0:T(8,128)} %copy-done.6, ...), custom_call_target="tpu_custom_call" | custom-call | flops 10066329600 | bytes 32768000 | tf_op jit(solution)/shard_map/ladder_product/pallas_call | solution.py:60
  183.3 0.4 collective-permute-start.33
  183.7 16.9 %collective-permute-done.28 = f32[64,2560]{1,0:T(8,128)S(1)} collective-permute-done((f32[64,2560]{1,0:T(8,128)}, f32[64,2560]{1,0:T(8,128)S(1)}, u32[]{:S(2)}, u32[]{:S(2)}) %collective-permute-start.28) | collective-permute-done | bytes 655392 | tf_op jit(solution)/shard_map/ppermute | solution.py:78
  200.6 0.4 collective-permute-done.27
  201.0 1.4 add_add_fusion.1
  202.5 1.2 slice_add_fusion
  203.7 2.9 %collective-permute-start.34 = (f32[64,2560]{1,0:T(8,128)S(1)}, f32[64,2560]{1,0:T(8,128)S(1)}, u32[]{:S(2)}, u32[]{:S(2)}) collective-permute-start(f32[64,2560]{1,0:T(8,128)S(1)} %slice_add_fusion), channel_id=1, source_target_pairs={{0,16},{8,24},{16,0},{24,8},{1,17},{9,25},{17,1},{25,9},{2,18},{10... | collective-permute-start | bytes 1966088 | tf_op jit(solution)/shard_map/ppermute | solution.py:78
  206.6 17.3 %ladder_product.9 = (f32[128,1280]{1,0:T(8,128)}, f32[128,1280]{1,0:T(8,128)}) custom-call(s32[8]{0:T(128)} %fusion.2.place_ref, f32[32,5120]{1,0:T(8,128)} %copy-done, f32[32,5120]{1,0:T(8,128)} %copy-done.4, f32[32,5120]{1,0:T(8,128)} %copy-done.3, f32[32,5120]{1,0:T(8,128)} %copy-done.5, f32[32,5120]{1,0:T(8,128)} %copy-done.2, f32[32,5120]{1,0:T(8,128)} %copy-done.6, ...), custom_call_target="tpu_custom_call" | custom-call | flops 10066329600 | bytes 32768000 | tf_op jit(solution)/shard_map/ladder_product/pallas_call | solution.py:60
  224.0 1.0 divide_dynamic-update-slice_fusion.1
  225.0 8.5 %collective-permute-done.34 = f32[64,2560]{1,0:T(8,128)S(1)} collective-permute-done((f32[64,2560]{1,0:T(8,128)S(1)}, f32[64,2560]{1,0:T(8,128)S(1)}, u32[]{:S(2)}, u32[]{:S(2)}) %collective-permute-start.34) | collective-permute-done | bytes 655392 | tf_op jit(solution)/shard_map/ppermute | solution.py:78
  233.7 1.2 add_add_fusion
  234.9 14.4 %collective-permute-done.36 = f32[128,1280]{1,0:T(8,128)S(1)} collective-permute-done((f32[128,1280]{1,0:T(8,128)}, f32[128,1280]{1,0:T(8,128)S(1)}, u32[]{:S(2)}, u32[]{:S(2)}) %collective-permute-start.36) | collective-permute-done | bytes 655392 | tf_op jit(solution)/shard_map/ppermute | solution.py:78
  249.3 1.0 collective-permute-start.37
  250.3 1.0 divide_dynamic-update-slice_fusion
  251.4 0.8 divide_dynamic-update-slice_fusion.3
  252.2 11.6 %collective-permute-done.37 = f32[64,1280]{1,0:T(8,128)S(1)} collective-permute-done((f32[64,1280]{1,0:T(8,128)S(1)}, f32[64,1280]{1,0:T(8,128)S(1)}, u32[]{:S(2)}, u32[]{:S(2)}) %collective-permute-start.37) | collective-permute-done | bytes 327712 | tf_op jit(solution)/shard_map/ppermute | solution.py:78
  263.9 0.8 divide_dynamic-update-slice_fusion.2
  (106 shorter events, 1.2 us)
Async XLA Ops:
  1.1 39.5 %copy-start.11 = (f32[32,5120]{1,0:T(8,128)}, f32[32,5120]{1,0:T(8,128)S(1)}, u32[]{:S(2)}) copy-start(f32[32,5120]{1,0:T(8,128)S(1)} %slice.91.refs_0_) | copy-start | bytes 1966084
  1.1 19.6 %collective-permute-start.2 = (f32[32,5120]{1,0:T(8,128)S(1)}, f32[32,5120]{1,0:T(8,128)S(1)}, u32[]{:S(2)}, u32[]{:S(2)}) collective-permute-start(f32[32,5120]{1,0:T(8,128)S(1)} %slice.91.refs_0_), channel_id=1, source_target_pairs={{0,6},{1,7},{2,4},{3,5},{4,2},{5,3},{6,0},{7,1},{8,14},{9,15},{10,... | collective-permute-start | bytes 1966088 | tf_op jit(solution)/shard_map/ppermute | solution.py:78
  5.1 28.8 %collective-permute-start.1 = (f32[32,5120]{1,0:T(8,128)S(1)}, f32[32,5120]{1,0:T(8,128)S(1)}, u32[]{:S(2)}, u32[]{:S(2)}) collective-permute-start(f32[32,5120]{1,0:T(8,128)S(1)} %slice.91.refs_0_), channel_id=1, source_target_pairs={{0,4},{1,5},{2,6},{3,7},{4,0},{5,1},{6,2},{7,3},{8,12},{9,13},{10,... | collective-permute-start | bytes 1966088 | tf_op jit(solution)/shard_map/ppermute | solution.py:78
  5.6 28.7 %collective-permute-start = (f32[32,5120]{1,0:T(8,128)S(1)}, f32[32,5120]{1,0:T(8,128)}, u32[]{:S(2)}, u32[]{:S(2)}) collective-permute-start(f32[32,5120]{1,0:T(8,128)S(1)} %slice.91.refs_0_), channel_id=1, source_target_pairs={{0,2},{1,3},{2,0},{3,1},{4,6},{5,7},{6,4},{7,5},{8,10},{9,11},{10,... | collective-permute-start | bytes 1966088 | tf_op jit(solution)/shard_map/ppermute | solution.py:78
  5.8 32.2 %collective-permute-start.3 = (f32[32,5120]{1,0:T(8,128)S(1)}, f32[32,5120]{1,0:T(8,128)}, u32[]{:S(2)}, u32[]{:S(2)}) collective-permute-start(f32[32,5120]{1,0:T(8,128)S(1)} %slice.91.refs_0_), channel_id=1, source_target_pairs={{0,1},{1,0},{2,3},{3,2},{4,5},{5,4},{6,7},{7,6},{8,9},{9,8},{10,11... | collective-permute-start | bytes 1966088 | tf_op jit(solution)/shard_map/ppermute | solution.py:78
  20.7 19.9 %copy-start.24 = (f32[32,5120]{1,0:T(8,128)}, f32[32,5120]{1,0:T(8,128)S(1)}, u32[]{:S(2)}) copy-start(f32[32,5120]{1,0:T(8,128)S(1)} %collective-permute-done.2.refs_6_) | copy-start | bytes 1966084
  20.7 18.5 %collective-permute-start.6 = (f32[32,5120]{1,0:T(8,128)S(1)}, f32[32,5120]{1,0:T(8,128)S(1)}, u32[]{:S(2)}, u32[]{:S(2)}) collective-permute-start(f32[32,5120]{1,0:T(8,128)S(1)} %collective-permute-done.2.refs_6_), channel_id=1, source_target_pairs={{0,1},{1,0},{2,3},{3,2},{4,5},{5,4},{6,7},{7,6},{8,9},{9,8},{10,11... | collective-permute-start | bytes 1966088 | tf_op jit(solution)/shard_map/ppermute | solution.py:78
  33.9 6.8 %copy-start.25 = (f32[32,5120]{1,0:T(8,128)}, f32[32,5120]{1,0:T(8,128)S(1)}, u32[]{:S(2)}) copy-start(f32[32,5120]{1,0:T(8,128)S(1)} %collective-permute-done.1.refs_4_) | copy-start | bytes 1966084
  33.9 5.8 %collective-permute-start.5 = (f32[32,5120]{1,0:T(8,128)S(1)}, f32[32,5120]{1,0:T(8,128)S(1)}, u32[]{:S(2)}, u32[]{:S(2)}) collective-permute-start(f32[32,5120]{1,0:T(8,128)S(1)} %collective-permute-done.1.refs_4_), channel_id=1, source_target_pairs={{0,1},{1,0},{2,3},{3,2},{4,5},{5,4},{6,7},{7,6},{8,9},{9,8},{10,11... | collective-permute-start | bytes 1966088 | tf_op jit(solution)/shard_map/ppermute | solution.py:78
  34.3 5.4 %collective-permute-start.4 = (f32[32,5120]{1,0:T(8,128)}, f32[32,5120]{1,0:T(8,128)S(1)}, u32[]{:S(2)}, u32[]{:S(2)}) collective-permute-start(f32[32,5120]{1,0:T(8,128)} %collective-permute-done.refs_2_), channel_id=1, source_target_pairs={{0,1},{1,0},{2,3},{3,2},{4,5},{5,4},{6,7},{7,6},{8,9},{9,8},{10,11... | collective-permute-start | bytes 1966088 | tf_op jit(solution)/shard_map/ppermute | solution.py:78
  36.0 34.1 %copy-start.15 = (f32[32,5120]{1,0:T(8,128)}, f32[32,5120]{1,0:T(8,128)S(1)}, u32[]{:S(2)}) copy-start(f32[32,5120]{1,0:T(8,128)S(1)} %get-tuple-element.75.refs_0_) | copy-start | bytes 1966084
  36.0 40.9 %copy-start.14 = (f32[32,5120]{1,0:T(8,128)}, f32[32,5120]{1,0:T(8,128)S(1)}, u32[]{:S(2)}) copy-start(f32[32,5120]{1,0:T(8,128)S(1)} %get-tuple-element.74.refs_0_) | copy-start | bytes 1966084
  36.0 118.4 %copy-start = (f32[32,5120]{1,0:T(8,128)}, f32[32,5120]{1,0:T(8,128)S(1)}, u32[]{:S(2)}) copy-start(f32[32,5120]{1,0:T(8,128)S(1)} %get-tuple-element.84.refs_0_) | copy-start | bytes 1966084
  36.0 34.0 %collective-permute-start.9 = (f32[32,5120]{1,0:T(8,128)S(1)}, f32[32,5120]{1,0:T(8,128)S(1)}, u32[]{:S(2)}, u32[]{:S(2)}) collective-permute-start(f32[32,5120]{1,0:T(8,128)S(1)} %get-tuple-element.75.refs_0_), channel_id=1, source_target_pairs={{0,6},{1,7},{2,4},{3,5},{4,2},{5,3},{6,0},{7,1},{8,14},{9,15},{10,... | collective-permute-start | bytes 1966088 | tf_op jit(solution)/shard_map/ppermute | solution.py:78
  37.9 32.2 %collective-permute-start.8 = (f32[32,5120]{1,0:T(8,128)S(1)}, f32[32,5120]{1,0:T(8,128)}, u32[]{:S(2)}, u32[]{:S(2)}) collective-permute-start(f32[32,5120]{1,0:T(8,128)S(1)} %get-tuple-element.75.refs_0_), channel_id=1, source_target_pairs={{0,4},{1,5},{2,6},{3,7},{4,0},{5,1},{6,2},{7,3},{8,12},{9,13},{10,... | collective-permute-start | bytes 1966088 | tf_op jit(solution)/shard_map/ppermute | solution.py:78
  39.3 1.4 copy-start.29
  39.3 30.9 %collective-permute-start.7 = (f32[32,5120]{1,0:T(8,128)S(1)}, f32[32,5120]{1,0:T(8,128)}, u32[]{:S(2)}, u32[]{:S(2)}) collective-permute-start(f32[32,5120]{1,0:T(8,128)S(1)} %get-tuple-element.75.refs_0_), channel_id=1, source_target_pairs={{0,2},{1,3},{2,0},{3,1},{4,6},{5,7},{6,4},{7,5},{8,10},{9,11},{10,... | collective-permute-start | bytes 1966088 | tf_op jit(solution)/shard_map/ppermute | solution.py:78
  39.6 1.1 copy-start.30
  40.5 30.7 %copy-start.16 = (s32[2560]{0:T(1024)S(1)}, s32[2560]{0:T(1024)}, u32[]{:S(2)}) copy-start(s32[2560]{0:T(1024)} %param.15) | copy-start | bytes 30724
  40.5 30.7 %copy-start.17 = (s32[2560]{0:T(1024)S(1)}, s32[2560]{0:T(1024)}, u32[]{:S(2)}) copy-start(s32[2560]{0:T(1024)} %param.14) | copy-start | bytes 30724
  40.5 30.7 %copy-start.18 = (f32[256]{0:T(256)S(1)}, f32[256]{0:T(256)}, u32[]{:S(2)}) copy-start(f32[256]{0:T(256)} %param.11) | copy-start | bytes 3076
  40.5 33.1 %copy-start.19 = (s32[256]{0:T(256)S(1)}, s32[256]{0:T(256)}, u32[]{:S(2)}) copy-start(s32[256]{0:T(256)} %param.13) | copy-start | bytes 3076
  40.5 33.1 %copy-start.20 = (s32[256]{0:T(256)S(1)}, s32[256]{0:T(256)}, u32[]{:S(2)}) copy-start(s32[256]{0:T(256)} %param.12) | copy-start | bytes 3076
  40.6 33.1 %copy-start.21 = (f32[64]{0:T(128)S(1)}, f32[64]{0:T(128)}, u32[]{:S(2)}) copy-start(f32[64]{0:T(128)} %param.10) | copy-start | bytes 772
  40.6 33.2 %collective-permute-start.14 = (f32[32,5120]{1,0:T(8,128)S(1)}, f32[32,5120]{1,0:T(8,128)}, u32[]{:S(2)}, u32[]{:S(2)}) collective-permute-start(f32[32,5120]{1,0:T(8,128)S(1)} %get-tuple-element.75.refs_0_), channel_id=1, source_target_pairs={{0,1},{1,0},{2,3},{3,2},{4,5},{5,4},{6,7},{7,6},{8,9},{9,8},{10,11... | collective-permute-start | bytes 1966088 | tf_op jit(solution)/shard_map/ppermute | solution.py:78
  70.1 10.2 %copy-start.23 = (f32[32,5120]{1,0:T(8,128)}, f32[32,5120]{1,0:T(8,128)S(1)}, u32[]{:S(2)}) copy-start(f32[32,5120]{1,0:T(8,128)S(1)} %collective-permute-done.9.refs_6_) | copy-start | bytes 1966084
  70.1 5.5 %collective-permute-start.15 = (f32[32,5120]{1,0:T(8,128)}, f32[32,5120]{1,0:T(8,128)S(1)}, u32[]{:S(2)}, u32[]{:S(2)}) collective-permute-start(f32[32,5120]{1,0:T(8,128)} %collective-permute-done.7.refs_2_), channel_id=1, source_target_pairs={{0,1},{1,0},{2,3},{3,2},{4,5},{5,4},{6,7},{7,6},{8,9},{9,8},{10,11... | collective-permute-start | bytes 1966088 | tf_op jit(solution)/shard_map/ppermute | solution.py:78
  70.7 6.3 %collective-permute-start.16 = (f32[32,5120]{1,0:T(8,128)}, f32[32,5120]{1,0:T(8,128)S(1)}, u32[]{:S(2)}, u32[]{:S(2)}) collective-permute-start(f32[32,5120]{1,0:T(8,128)} %collective-permute-done.8.refs_4_), channel_id=1, source_target_pairs={{0,1},{1,0},{2,3},{3,2},{4,5},{5,4},{6,7},{7,6},{8,9},{9,8},{10,11... | collective-permute-start | bytes 1966088 | tf_op jit(solution)/shard_map/ppermute | solution.py:78
  70.7 6.6 %collective-permute-start.17 = (f32[32,5120]{1,0:T(8,128)S(1)}, f32[32,5120]{1,0:T(8,128)S(1)}, u32[]{:S(2)}, u32[]{:S(2)}) collective-permute-start(f32[32,5120]{1,0:T(8,128)S(1)} %collective-permute-done.9.refs_6_), channel_id=1, source_target_pairs={{0,1},{1,0},{2,3},{3,2},{4,5},{5,4},{6,7},{7,6},{8,9},{9,8},{10,11... | collective-permute-start | bytes 1966088 | tf_op jit(solution)/shard_map/ppermute | solution.py:78
  71.2 40.7 %collective-permute-start.23 = (f32[32,5120]{1,0:T(8,128)S(1)}, f32[32,5120]{1,0:T(8,128)S(1)}, u32[]{:S(2)}, u32[]{:S(2)}) collective-permute-start(f32[32,5120]{1,0:T(8,128)S(1)} %get-tuple-element.74.refs_0_), channel_id=1, source_target_pairs={{0,1},{1,0},{2,3},{3,2},{4,5},{5,4},{6,7},{7,6},{8,9},{9,8},{10,11... | collective-permute-start | bytes 1966088 | tf_op jit(solution)/shard_map/ppermute | solution.py:78
  73.7 37.2 %copy-start.8 = (f32[128,2560]{1,0:T(8,128)S(1)}, f32[128,2560]{1,0:T(8,128)}, u32[]{:S(2)}) copy-start(f32[128,2560]{1,0:T(8,128)} %get-tuple-element.66) | copy-start | bytes 3932164
  73.8 36.0 %collective-permute-start.13 = (f32[32,5120]{1,0:T(8,128)S(1)}, f32[32,5120]{1,0:T(8,128)}, u32[]{:S(2)}, u32[]{:S(2)}) collective-permute-start(f32[32,5120]{1,0:T(8,128)S(1)} %get-tuple-element.74.refs_0_), channel_id=1, source_target_pairs={{0,6},{1,7},{2,4},{3,5},{4,2},{5,3},{6,0},{7,1},{8,14},{9,15},{10,... | collective-permute-start | bytes 1966088 | tf_op jit(solution)/shard_map/ppermute | solution.py:78
  75.6 1.8 copy-start.26
  75.6 34.6 %collective-permute-start.12 = (f32[32,5120]{1,0:T(8,128)S(1)}, f32[32,5120]{1,0:T(8,128)}, u32[]{:S(2)}, u32[]{:S(2)}) collective-permute-start(f32[32,5120]{1,0:T(8,128)S(1)} %get-tuple-element.74.refs_0_), channel_id=1, source_target_pairs={{0,4},{1,5},{2,6},{3,7},{4,0},{5,1},{6,2},{7,3},{8,12},{9,13},{10,... | collective-permute-start | bytes 1966088 | tf_op jit(solution)/shard_map/ppermute | solution.py:78
  76.9 33.3 %collective-permute-start.11 = (f32[32,5120]{1,0:T(8,128)S(1)}, f32[32,5120]{1,0:T(8,128)}, u32[]{:S(2)}, u32[]{:S(2)}) collective-permute-start(f32[32,5120]{1,0:T(8,128)S(1)} %get-tuple-element.74.refs_0_), channel_id=1, source_target_pairs={{0,2},{1,3},{2,0},{3,1},{4,6},{5,7},{6,4},{7,5},{8,10},{9,11},{10,... | collective-permute-start | bytes 1966088 | tf_op jit(solution)/shard_map/ppermute | solution.py:78
  78.7 31.5 %collective-permute-start.10 = (f32[128,2560]{1,0:T(8,128)}, f32[128,2560]{1,0:T(8,128)S(1)}, u32[]{:S(2)}, u32[]{:S(2)}) collective-permute-start(f32[128,2560]{1,0:T(8,128)} %get-tuple-element.67), channel_id=1, source_target_pairs={{0,8},{8,0},{16,24},{24,16},{1,9},{9,1},{17,25},{25,17},{2,10},{10... | collective-permute-start | bytes 3932168 | tf_op jit(solution)/shard_map/ppermute | solution.py:78
  109.7 44.7 %collective-permute-start.18 = (f32[128,2560]{1,0:T(8,128)}, f32[128,2560]{1,0:T(8,128)}, u32[]{:S(2)}, u32[]{:S(2)}) collective-permute-start(f32[128,2560]{1,0:T(8,128)} %get-tuple-element.80), channel_id=1, source_target_pairs={{0,8},{8,0},{16,24},{24,16},{1,9},{9,1},{17,25},{25,17},{2,10},{10... | collective-permute-start | bytes 3932168 | tf_op jit(solution)/shard_map/ppermute | solution.py:78
  110.3 3.0 %collective-permute-start.24 = (f32[32,5120]{1,0:T(8,128)}, f32[32,5120]{1,0:T(8,128)}, u32[]{:S(2)}, u32[]{:S(2)}) collective-permute-start(f32[32,5120]{1,0:T(8,128)} %collective-permute-done.11.refs_2_), channel_id=1, source_target_pairs={{0,1},{1,0},{2,3},{3,2},{4,5},{5,4},{6,7},{7,6},{8,9},{9,8},{10,11... | collective-permute-start | bytes 1966088 | tf_op jit(solution)/shard_map/ppermute | solution.py:78
  110.4 4.2 %collective-permute-start.25 = (f32[32,5120]{1,0:T(8,128)}, f32[32,5120]{1,0:T(8,128)}, u32[]{:S(2)}, u32[]{:S(2)}) collective-permute-start(f32[32,5120]{1,0:T(8,128)} %collective-permute-done.12.refs_4_), channel_id=1, source_target_pairs={{0,1},{1,0},{2,3},{3,2},{4,5},{5,4},{6,7},{7,6},{8,9},{9,8},{10,11... | collective-permute-start | bytes 1966088 | tf_op jit(solution)/shard_map/ppermute | solution.py:78
  110.9 4.5 %collective-permute-start.26 = (f32[32,5120]{1,0:T(8,128)}, f32[32,5120]{1,0:T(8,128)}, u32[]{:S(2)}, u32[]{:S(2)}) collective-permute-start(f32[32,5120]{1,0:T(8,128)} %collective-permute-done.13.refs_6_), channel_id=1, source_target_pairs={{0,1},{1,0},{2,3},{3,2},{4,5},{5,4},{6,7},{7,6},{8,9},{9,8},{10,11... | collective-permute-start | bytes 1966088 | tf_op jit(solution)/shard_map/ppermute | solution.py:78
  111.9 6.1 %copy-start.22 = (f32[32,5120]{1,0:T(8,128)}, f32[32,5120]{1,0:T(8,128)S(1)}, u32[]{:S(2)}) copy-start(f32[32,5120]{1,0:T(8,128)S(1)} %collective-permute-done.23.refs_1_) | copy-start | bytes 1966084
  111.9 45.2 %collective-permute-start.21 = (f32[32,5120]{1,0:T(8,128)S(1)}, f32[32,5120]{1,0:T(8,128)S(1)}, u32[]{:S(2)}, u32[]{:S(2)}) collective-permute-start(f32[32,5120]{1,0:T(8,128)S(1)} %get-tuple-element.84.refs_0_), channel_id=1, source_target_pairs={{0,6},{1,7},{2,4},{3,5},{4,2},{5,3},{6,0},{7,1},{8,14},{9,15},{10,... | collective-permute-start | bytes 1966088 | tf_op jit(solution)/shard_map/ppermute | solution.py:78
  113.4 43.7 %collective-permute-start.20 = (f32[32,5120]{1,0:T(8,128)S(1)}, f32[32,5120]{1,0:T(8,128)S(1)}, u32[]{:S(2)}, u32[]{:S(2)}) collective-permute-start(f32[32,5120]{1,0:T(8,128)S(1)} %get-tuple-element.84.refs_0_), channel_id=1, source_target_pairs={{0,4},{1,5},{2,6},{3,7},{4,0},{5,1},{6,2},{7,3},{8,12},{9,13},{10,... | collective-permute-start | bytes 1966088 | tf_op jit(solution)/shard_map/ppermute | solution.py:78
  114.6 42.5 %collective-permute-start.19 = (f32[32,5120]{1,0:T(8,128)S(1)}, f32[32,5120]{1,0:T(8,128)S(1)}, u32[]{:S(2)}, u32[]{:S(2)}) collective-permute-start(f32[32,5120]{1,0:T(8,128)S(1)} %get-tuple-element.84.refs_0_), channel_id=1, source_target_pairs={{0,2},{1,3},{2,0},{3,1},{4,6},{5,7},{6,4},{7,5},{8,10},{9,11},{10,... | collective-permute-start | bytes 1966088 | tf_op jit(solution)/shard_map/ppermute | solution.py:78
  115.4 39.1 %collective-permute-start.22 = (f32[64,2560]{1,0:T(8,128)}, f32[64,2560]{1,0:T(8,128)}, u32[]{:S(2)}, u32[]{:S(2)}) collective-permute-start(f32[64,2560]{1,0:T(8,128)} %slice_add_fusion.2), channel_id=1, source_target_pairs={{0,16},{8,24},{16,0},{24,8},{1,17},{9,25},{17,1},{25,9},{2,18},{10... | collective-permute-start | bytes 1966088 | tf_op jit(solution)/shard_map/ppermute | solution.py:78
  154.5 9.0 %collective-permute-start.29 = (f32[32,5120]{1,0:T(8,128)S(1)}, f32[32,5120]{1,0:T(8,128)S(1)}, u32[]{:S(2)}, u32[]{:S(2)}) collective-permute-start(f32[32,5120]{1,0:T(8,128)S(1)} %get-tuple-element.84.refs_0_), channel_id=1, source_target_pairs={{0,1},{1,0},{2,3},{3,2},{4,5},{5,4},{6,7},{7,6},{8,9},{9,8},{10,11... | collective-permute-start | bytes 1966088 | tf_op jit(solution)/shard_map/ppermute | solution.py:78
  154.5 46.6 %collective-permute-start.27 = (f32[128,2560]{1,0:T(8,128)}, f32[128,2560]{1,0:T(8,128)}, u32[]{:S(2)}, u32[]{:S(2)}) collective-permute-start(f32[128,2560]{1,0:T(8,128)} %get-tuple-element.89), channel_id=1, source_target_pairs={{0,8},{8,0},{16,24},{24,16},{1,9},{9,1},{17,25},{25,17},{2,10},{10... | collective-permute-start | bytes 3932168 | tf_op jit(solution)/shard_map/ppermute | solution.py:78
  157.0 4.3 %copy-start.1 = (f32[32,5120]{1,0:T(8,128)}, f32[32,5120]{1,0:T(8,128)S(1)}, u32[]{:S(2)}) copy-start(f32[32,5120]{1,0:T(8,128)S(1)} %collective-permute-done.21.refs_6_) | copy-start | bytes 1966084
  157.1 4.3 %copy-start.2 = (f32[32,5120]{1,0:T(8,128)}, f32[32,5120]{1,0:T(8,128)S(1)}, u32[]{:S(2)}) copy-start(f32[32,5120]{1,0:T(8,128)S(1)} %collective-permute-done.20.refs_4_) | copy-start | bytes 1966084
  157.1 4.3 %copy-start.3 = (f32[32,5120]{1,0:T(8,128)}, f32[32,5120]{1,0:T(8,128)S(1)}, u32[]{:S(2)}) copy-start(f32[32,5120]{1,0:T(8,128)S(1)} %collective-permute-done.19.refs_2_) | copy-start | bytes 1966084
  158.8 2.6 copy-start.9
  158.8 5.2 %collective-permute-start.30 = (f32[32,5120]{1,0:T(8,128)S(1)}, f32[32,5120]{1,0:T(8,128)S(1)}, u32[]{:S(2)}, u32[]{:S(2)}) collective-permute-start(f32[32,5120]{1,0:T(8,128)S(1)} %collective-permute-done.19.refs_2_), channel_id=1, source_target_pairs={{0,1},{1,0},{2,3},{3,2},{4,5},{5,4},{6,7},{7,6},{8,9},{9,8},{10,11... | collective-permute-start | bytes 1966088 | tf_op jit(solution)/shard_map/ppermute | solution.py:78
  158.9 5.1 %collective-permute-start.31 = (f32[32,5120]{1,0:T(8,128)S(1)}, f32[32,5120]{1,0:T(8,128)S(1)}, u32[]{:S(2)}, u32[]{:S(2)}) collective-permute-start(f32[32,5120]{1,0:T(8,128)S(1)} %collective-permute-done.20.refs_4_), channel_id=1, source_target_pairs={{0,1},{1,0},{2,3},{3,2},{4,5},{5,4},{6,7},{7,6},{8,9},{9,8},{10,11... | collective-permute-start | bytes 1966088 | tf_op jit(solution)/shard_map/ppermute | solution.py:78
  159.4 4.7 %collective-permute-start.32 = (f32[32,5120]{1,0:T(8,128)S(1)}, f32[32,5120]{1,0:T(8,128)S(1)}, u32[]{:S(2)}, u32[]{:S(2)}) collective-permute-start(f32[32,5120]{1,0:T(8,128)S(1)} %collective-permute-done.21.refs_6_), channel_id=1, source_target_pairs={{0,1},{1,0},{2,3},{3,2},{4,5},{5,4},{6,7},{7,6},{8,9},{9,8},{10,11... | collective-permute-start | bytes 1966088 | tf_op jit(solution)/shard_map/ppermute | solution.py:78
  163.4 37.2 %collective-permute-start.28 = (f32[64,2560]{1,0:T(8,128)}, f32[64,2560]{1,0:T(8,128)S(1)}, u32[]{:S(2)}, u32[]{:S(2)}) collective-permute-start(f32[64,2560]{1,0:T(8,128)} %slice_add_fusion.1), channel_id=1, source_target_pairs={{0,16},{8,24},{16,0},{24,8},{1,17},{9,25},{17,1},{25,9},{2,18},{10... | collective-permute-start | bytes 1966088 | tf_op jit(solution)/shard_map/ppermute | solution.py:78
  164.0 1.1 copy-start.6
  183.3 19.1 %copy-start.10 = (f32[128,2560]{1,0:T(8,128)S(1)}, f32[128,2560]{1,0:T(8,128)}, u32[]{:S(2)}) copy-start(f32[128,2560]{1,0:T(8,128)} %get-tuple-element.88) | copy-start | bytes 3932164
  183.3 41.7 %collective-permute-start.33 = (f32[128,1280]{1,0:T(8,128)}, f32[128,1280]{1,0:T(8,128)S(1)}, u32[]{:S(2)}, u32[]{:S(2)}) collective-permute-start(f32[128,1280]{1,0:T(8,128)} %get-tuple-element.99), channel_id=1, source_target_pairs={{0,8},{8,0},{16,24},{24,16},{1,9},{9,1},{17,25},{25,17},{2,10},{10... | collective-permute-start | bytes 1966088 | tf_op jit(solution)/shard_map/ppermute | solution.py:78
  203.6 29.9 %copy-start.12 = (f32[128,1280]{1,0:T(8,128)S(1)}, f32[128,1280]{1,0:T(8,128)}, u32[]{:S(2)}) copy-start(f32[128,1280]{1,0:T(8,128)} %get-tuple-element.98) | copy-start | bytes 1966084
  203.7 29.9 %collective-permute-start.34 = (f32[64,2560]{1,0:T(8,128)S(1)}, f32[64,2560]{1,0:T(8,128)S(1)}, u32[]{:S(2)}, u32[]{:S(2)}) collective-permute-start(f32[64,2560]{1,0:T(8,128)S(1)} %slice_add_fusion), channel_id=1, source_target_pairs={{0,16},{8,24},{16,0},{24,8},{1,17},{9,25},{17,1},{25,9},{2,18},{10... | collective-permute-start | bytes 1966088 | tf_op jit(solution)/shard_map/ppermute | solution.py:78
  223.9 25.3 %copy-start.13 = (f32[128,1280]{1,0:T(8,128)S(1)}, f32[128,1280]{1,0:T(8,128)}, u32[]{:S(2)}) copy-start(f32[128,1280]{1,0:T(8,128)} %get-tuple-element.103) | copy-start | bytes 1966084
  223.9 25.3 %collective-permute-start.36 = (f32[128,1280]{1,0:T(8,128)}, f32[128,1280]{1,0:T(8,128)S(1)}, u32[]{:S(2)}, u32[]{:S(2)}) collective-permute-start(f32[128,1280]{1,0:T(8,128)} %get-tuple-element.104), channel_id=1, source_target_pairs={{0,8},{8,0},{16,24},{24,16},{1,9},{9,1},{17,25},{25,17},{2,10},{10... | collective-permute-start | bytes 1966088 | tf_op jit(solution)/shard_map/ppermute | solution.py:78
  233.6 17.7 %collective-permute-start.35 = (f32[64,1280]{1,0:T(8,128)S(1)}, f32[64,1280]{1,0:T(8,128)S(1)}, u32[]{:S(2)}, u32[]{:S(2)}) collective-permute-start(f32[64,1280]{1,0:T(8,128)S(1)} %slice_add_fusion.5), channel_id=1, source_target_pairs={{0,16},{8,24},{16,0},{24,8},{1,17},{9,25},{17,1},{25,9},{2,18},{10... | collective-permute-start | bytes 983048 | tf_op jit(solution)/shard_map/ppermute | solution.py:78
  249.3 14.6 %collective-permute-start.37 = (f32[64,1280]{1,0:T(8,128)S(1)}, f32[64,1280]{1,0:T(8,128)S(1)}, u32[]{:S(2)}, u32[]{:S(2)}) collective-permute-start(f32[64,1280]{1,0:T(8,128)S(1)} %slice_add_fusion.3), channel_id=1, source_target_pairs={{0,16},{8,24},{16,0},{24,8},{1,17},{9,25},{17,1},{25,9},{2,18},{10... | collective-permute-start | bytes 983048 | tf_op jit(solution)/shard_map/ppermute | solution.py:78
  (6 other events, 5.2 us)
